TPU v7x, 32 devices: a whole 2x2x4 slice. The times are simulated.
32 devices in a mesh: seq: 16 (over z, y, x), head: 2 (over core).
Axes of the slice: x: 2, y: 2, z: 4, core: 2. Of those that a mesh axis runs over, the one named last changes fastest.
Arguments:
- inner_acts: bfloat16 [4096, 8192], P('seq', 'head'), may hold values from -0.4375 to 0.4375
- out_grad: bfloat16 [4096, 8192], P('seq', 'head'), may hold values from -0.4375 to 0.4375
- write_proj: bfloat16 [4096, 128], P('seq'), may hold values from -3 to 3
- read_proj: bfloat16 [4096, 128], P('seq'), may hold values from -3 to 3
- log_decay: float32 [4096, 64], P('seq', 'head'), may hold values from -2.5 to 0, as said below
- w_in: bfloat16 [4096, 8192], P('seq', 'head'), may hold values from -0.09375 to 0.09375
Outputs:
- input_grad: bfloat16 [4096, 4096], P('seq', 'head')
- act_grad: bfloat16 [4096, 8192], P('seq', 'head')
- write_grad: float32 [4096, 128], P('seq')
- read_grad: float32 [4096, 128], P('seq')
Inputs may be any that keep to these rules, and one draw needn't show every extreme that they name: `log_decay`: natural log of a decay factor of each head at each token; every entry is negative.
All inputs are finite; a program needn't handle non-finite values.
Results may differ from a plain program's by a relative error of at most 0.019.
Values may be sent and summed in bfloat16 or wider, within the bound.
No kernel may reach another device: no remote copies, remote signals or barrier semaphores. Data moves between devices by JAX's collectives and lax.ppermute only.
A program may use at most 192 MiB of HBM per device.

v0:
```python
import jax
import jax.numpy as jnp
from jax import lax
from jax.sharding import PartitionSpec as P

SPAN = 256


exact_mode = lax.Precision.HIGHEST


def carried_in(shard, axis, combine, identity):
    devices, position = (lax.axis_size(axis), lax.axis_index(axis))
    everything = jax.tree.map(
        lambda part, kind: lax.all_gather(part.astype(kind), axis),
        shard,
        (jnp.bfloat16, jnp.bfloat16),
    )
    start = jax.tree.map(
        lambda part, zero: jnp.broadcast_to(jnp.asarray(zero, part.dtype), part.shape),
        shard,
        identity,
    )

    def step(k, before):
        reached = k < position
        new = combine(
            before, jax.tree.map(lambda part, own: part[k].astype(own.dtype), everything, shard)
        )
        return jax.tree.map(lambda a, b: jnp.where(reached, a, b), new, before)

    return lax.fori_loop(0, devices, step, start)


def carried_in_2(part, axis, combine, identity):
    count = lax.axis_size(axis)
    place = lax.axis_index(axis)
    ahead = count - 1 - place
    gathered = jax.tree.map(lambda a: lax.all_gather(a, axis), part)
    state = jax.tree.map(lambda a, e: jnp.zeros_like(a) + jnp.asarray(e, a.dtype), part, identity)

    def one(step, state):
        source = count - 1 - step
        return combine(
            state, jax.tree.map(lambda a: lax.dynamic_index_in_dim(a, source, 0, False), gathered)
        )

    return lax.fori_loop(0, ahead, one, state)


def decay_blocks(cumulative):
    count = cumulative.shape[1]
    by_head = jnp.swapaxes(cumulative, 1, 2)
    spread_log = by_head[:, :, :, None] - by_head[:, :, None, :]
    below_diag = jnp.arange(count)[:, None] >= jnp.arange(count)[None, :]
    return jnp.exp(jnp.where(below_diag, spread_log, -jnp.inf))


def combine(earlier, later):
    return (earlier[0] + later[0], jnp.exp(later[0])[:, None, None] * earlier[1] + later[1])


def local(inner_acts, out_grad, write_proj, read_proj, log_decay, w_in):
    tok_rows = inner_acts.shape[0]
    head_count = log_decay.shape[1]
    head_dim = inner_acts.shape[1] // head_count
    state_dim = write_proj.shape[1]
    blocks = tok_rows // SPAN
    act_narrow = inner_acts.reshape(blocks, SPAN, head_count, head_dim)
    grad_narrow = out_grad.reshape(blocks, SPAN, head_count, head_dim)
    act_blocks = act_narrow.astype(jnp.float32)
    grad_blocks = grad_narrow.astype(jnp.float32)
    write_blocks = write_proj.astype(jnp.float32).reshape(blocks, SPAN, state_dim)
    read_blocks = read_proj.astype(jnp.float32).reshape(blocks, SPAN, state_dim)
    cumulative = jnp.cumsum(log_decay.reshape(blocks, SPAN, head_count), axis=1)
    totals = cumulative[:, -1, :]
    tail_decay = jnp.exp(totals[:, None, :] - cumulative)
    head_decay = jnp.exp(cumulative)
    decays = decay_blocks(cumulative)
    weighted = decays * jnp.einsum(
        "kahp,kbhp->khab", grad_narrow, act_narrow, preferred_element_type=jnp.float32
    )
    read_local = jnp.einsum("khab,kbn->kan", weighted, write_blocks, precision=exact_mode)
    write_local = jnp.einsum("khab,kan->kbn", weighted, read_blocks, precision=exact_mode)
    scores = jnp.einsum(
        "kan,kbn->kab",
        read_proj.reshape(blocks, SPAN, state_dim),
        write_proj.reshape(blocks, SPAN, state_dim),
        preferred_element_type=jnp.float32,
    )
    act_local = jnp.einsum(
        "khab,kahp->kbhp", decays * scores[:, None], grad_blocks, precision=exact_mode
    )
    block_ends = jnp.einsum(
        "kbhp,kbn->khpn", act_blocks * tail_decay[..., None], write_blocks, precision=exact_mode
    )
    fronts = jnp.einsum(
        "kahp,kan->khpn", grad_blocks * head_decay[..., None], read_blocks, precision=exact_mode
    )
    zero_log = jnp.zeros((head_count,), jnp.float32)
    zero_state = jnp.zeros((head_count, head_dim, state_dim), jnp.float32)
    prefix_logs = []
    prefix_states = []
    running = (zero_log, zero_state)
    index = 0
    prefix_logs.append(running[0])
    prefix_states.append(running[1])
    running = combine(running, (totals[index], block_ends[index]))
    end_log, end_state = running
    suffix_logs = [zero_log] * blocks
    suffix_grads = [zero_state] * blocks
    running = (zero_log, zero_state)
    for index in reversed(range(blocks)):
        suffix_logs[index] = running[0]
        suffix_grads[index] = running[1]
        running = combine(running, (totals[index], fronts[index]))
    front_log, front_state = running
    state_in = carried_in((end_log, end_state), "seq", combine, (zero_log, zero_state))[1]
    grad_in = carried_in_2((front_log, front_state), "seq", combine, (zero_log, zero_state))[1]
    current = state_in
    index = 0
    states_list = [current]
    grads_list = [zero_state] * blocks
    current = grad_in
    for index in reversed(range(blocks)):
        grads_list[index] = current
        current = jnp.exp(totals[index])[:, None, None] * current + fronts[index]
    state_stack = jnp.stack(states_list)
    grad_stack = jnp.stack(grads_list)
    read_carry = jnp.einsum(
        "kahp,khpn->kan", grad_blocks * head_decay[..., None], state_stack, precision=exact_mode
    )
    write_carry = jnp.einsum(
        "kbhp,khpn->kbn", act_blocks * tail_decay[..., None], grad_stack, precision=exact_mode
    )
    act_carry = (
        jnp.einsum("khpn,kbn->kbhp", grad_stack, write_blocks, precision=exact_mode)
        * tail_decay[..., None]
    )
    act_grad = (act_local + act_carry).astype(jnp.bfloat16).reshape(tok_rows, head_count * head_dim)
    write_part = (write_local + write_carry).reshape(tok_rows, state_dim)
    read_part = (read_local + read_carry).reshape(tok_rows, state_dim)
    write_grad, read_grad = (
        lax.psum(write_part.astype(jnp.bfloat16), "head").astype(jnp.float32),
        lax.psum(read_part.astype(jnp.bfloat16), "head").astype(jnp.float32),
    )
    group_term = lax.dot_general(
        act_grad,
        lax.all_gather(w_in, "seq", axis=0, tiled=True),
        (((1,), (1,)), ((), ())),
        preferred_element_type=jnp.float32,
    )
    input_grad = lax.psum_scatter(
        group_term.astype(jnp.bfloat16).astype(jnp.float32).astype(jnp.bfloat16),
        "head",
        scatter_dimension=1,
        tiled=True,
    )
    return (input_grad, act_grad, write_grad, read_grad)


def solution(mesh):
    return jax.shard_map(
        local,
        mesh=mesh,
        in_specs=(
            P("seq", "head"),
            P("seq", "head"),
            P("seq", None),
            P("seq", None),
            P("seq", "head"),
            P("seq", "head"),
        ),
        out_specs=(P("seq", "head"), P("seq", "head"), P("seq", None), P("seq", None)),
        check_vma=False,
    )
```

profile of v0, /device:TPU:1, one launch (start us, length us, event | category | flops | bytes accessed | tf_op | source)
XLA Modules:
  0.0 970.5 jit_solution(7822208719122437121)
XLA Ops:
  9.1 2.3 mul.136
  11.4 5.8 copy.80
  17.2 4.9 convert_multiply_fusion
  22.0 5.6 copy.87
  27.7 5.1 add_convert_fusion
  36.0 6.7 fusion.22
  43.7 34.8 %all-gather.3 = bf16[16,1,32]{2,1,0:T(2,128)(2,1)S(1)} all-gather(bf16[1,1,32]{2,1,0:T(2,128)(2,1)S(1)} %slice.19), channel_id=5, replica_groups=mesh['seq'=16,'head'=2] {'seq'}, dimensions={0}, use_global_device_ids=true | all-gather | bytes 1088 | tf_op jit(solution)/shard_map/all_gather | solution.py:15
  78.5 29.0 %all-gather = f32[16,1,32]{2,1,0:T(1,128)S(1)} all-gather(f32[1,1,32]{2,1,0:T(1,128)S(1)} %get-tuple-element.257), channel_id=2, replica_groups=mesh['seq'=16,'head'=2] {'seq'}, dimensions={0}, use_global_device_ids=true | all-gather | bytes 2176 | tf_op jit(solution)/shard_map/all_gather | solution.py:39
  107.7 8.6 fusion.1
  116.3 2.7 multiply_reduce_fusion
  119.0 107.5 %all-gather.12.cloned.1.call-done = bf16[512,128,128]{2,1,0:T(8,128)(2,1)} async-done(((bf16[32,128,128]{2,1,0:T(8,128)(2,1)}), bf16[512,128,128]{2,1,0:T(8,128)(2,1)}) %all-gather.12.cloned.1.call-update) | async-done | bytes 16777232 | tf_op jit(solution)/shard_map/all_gather | solution.py:15
  226.5 36.7 %while.29 = (s32[]{:T(128)}, f32[32,128,128]{2,1,0:T(8,128)S(1)}, s32[]{:T(128)}, bf16[16,32]{1,0:T(8,128)(2,1)S(1)}, bf16[16,32,128,128]{3,2,1,0:T(8,128)(2,1)}, /*index=5*/s32[]{:T(128)}, s32[]{:T(128)}) while((s32[]{:T(128)}, f32[32,128,128]{2,1,0:T(8,128)S(1)}, s32[]{:T(128)}, bf16[16,32]{1,0:T(8,128)(2,1)S(1)}, ...), condition=%wide.region_8.9_spmd.clone, body=%wide.region_7.8_spmd.clone.sunk | while | flops 2621476 | bytes 5243305 | solution.py:32
  233.2 2.2 fusion.57
  235.5 2.4 fusion.57
  237.9 2.4 fusion.57
  240.3 2.5 fusion.57
  247.4 2.2 fusion.57
  249.7 2.2 fusion.57
  251.9 2.2 fusion.57
  258.7 2.2 fusion.57
  263.2 8.7 fusion.25
  272.8 306.1 %all-gather.10.cloned.1.call-done = f32[512,128,128]{2,1,0:T(8,128)} async-done(((f32[32,128,128]{2,1,0:T(8,128)}), f32[512,128,128]{2,1,0:T(8,128)}) %all-gather.10.cloned.1.call-update) | async-done | bytes 33554448 | tf_op jit(solution)/shard_map/all_gather | solution.py:39
  579.1 31.9 %while.28 = (s32[]{:T(128)}, f32[32,128,128]{2,1,0:T(8,128)S(1)}, s32[]{:T(128)}, f32[16,32]{1,0:T(8,128)S(1)}, f32[16,32,128,128]{3,2,1,0:T(8,128)}, /*index=5*/s32[]{:T(128)}, s32[]{:T(128)}, s32[]{:T(128)}, s32[]{:T(128)}) while((s32[]{:T(128)}, f32[32,128,128]{2,1,0:T(8,128)S(1)}, s32[]{:T(128)}, f32[16,32]{1,0:T(8,128)S(1)}, ...), condition=%wide.region_3.4_spmd, body=%wide.region_2.3_spmd.sunk | while | flops 1048582 | bytes 6291987 | solution.py:48
  587.3 2.3 bitcast_add_fusion.6
  589.6 2.3 bitcast_add_fusion.6
  592.0 2.5 bitcast_add_fusion.6
  611.0 8.5 convolution_bitcast_fusion
  620.6 5.3 fusion.8
  626.0 304.8 %all-gather.8.cloned.1.call-done = bf16[4096,4096]{1,0:T(8,128)(2,1)} async-done(((bf16[256,4096]{1,0:T(8,128)(2,1)}), bf16[4096,4096]{1,0:T(8,128)(2,1)}) %all-gather.8.cloned.1.call-update) | async-done | bytes 33554448 | tf_op jit(solution)/shard_map/all_gather | solution.py:149
  930.8 16.9 %convolution_convert_fusion = bf16[256,4096]{1,0:T(8,128)(2,1)} fusion(bf16[256,4096]{0,1:T(8,128)(2,1)} %bitcast.143, bf16[4096,4096]{1,0:T(8,128)(2,1)} %all-gather.8.cloned.1.call-done), kind=kOutput, calls=%fused_computation.9 | convolution fusion | flops 8590983168 | bytes 37748736 | tf_op jit(solution)/shard_map/dot_general | solution.py:147
  949.3 2.8 copy.84
  955.2 8.8 reduce-scatter.2.cloned.1.call-done
  (105 shorter events, 54.8 us)
Async XLA Ops:
  7.2 20.5 %copy-start = (bf16[256,128]{1,0:T(8,128)(2,1)S(1)}, bf16[256,128]{1,0:T(8,128)(2,1)}, u32[]{:S(2)}) copy-start(bf16[256,128]{1,0:T(8,128)(2,1)} %param.12) | copy-start | bytes 196612
  7.2 219.3 %all-gather.12.cloned.1.call-start = ((), (), s32[]{:S(2)}) async-start(), calls=%async_computation.4 | async-start | bytes 17825792 | tf_op jit(solution)/shard_map/all_gather | solution.py:15
  11.4 5.8 copy-start.5
  32.8 546.1 %all-gather.10.cloned.1.call-start = ((), (), s32[]{:S(2)}) async-start(), calls=%async_computation.3 | async-start | bytes 35651584 | tf_op jit(solution)/shard_map/all_gather | solution.py:39
  32.9 3.1 copy-start.3
  32.9 3.1 copy-start.7
  34.0 2.0 copy-start.1
  42.7 888.0 %all-gather.8.cloned.1.call-start = ((), (), s32[]{:S(2)}) async-start(), calls=%async_computation.1 | async-start | bytes 35651584 | tf_op jit(solution)/shard_map/all_gather | solution.py:149
  43.5 908.7 %all-reduce.3.cloned.1.call-start = ((), (), s32[]{:S(2)}) async-start(), calls=%async_computation.5 | async-start | bytes 262144 | tf_op jit(solution)/shard_map/psum | solution.py:144
  107.7 8.6 copy-start.4
  107.7 8.6 copy-start.6
  625.9 338.0 %reduce-scatter.2.cloned.1.call-start = ((), (), s32[]{:S(2)}) async-start(), calls=%async_computation.2 | async-start | bytes 3145728 | tf_op jit(solution)/shard_map/reduce_scatter | solution.py:153
  947.7 1.6 copy-start.2
Sparse Core Ops, SparseCore 0:
  32.9 193.4 all-gather.11
  229.8 349.0 all-gather.9
  581.7 349.0 all-gather.7
  933.5 16.9 all-reduce.2
  953.2 10.7 reduce-scatter.1
where the time goes:
time: 972 us; the launch traced here: 970 us
  waiting for transfers between devices  728 us (75%)
  other arithmetic  75.7 us (8%)
  matrix products  64.7 us (7%)
  blocking collectives  63.8 us (7%)
  local copies, waits for them, and re-layouts  22.9 us (2%)
  between operations  14 us (1%)
    all_gather x1, waiting for transfers between devices, carried_in_2(): gathered = jax.tree.map(lambda a: lax.all_gather(a, axis), part)  306 us
    all_gather x1, waiting for transfers between devices, local(): lax.all_gather(w_in, 'seq', axis=0, tiled=True)  305 us
    all_gather x1, waiting for transfers between devices, carried_in(): lax.all_gather(part.astype(kind), axis)  107 us
    select_n x16, other arithmetic, step(): return jax.tree.map(lambda a, b: jnp.where(reached, a, b), new, before)  36 us
    all_gather x1, blocking collectives, carried_in(): lax.all_gather(part.astype(kind), axis)  34.8 us
    add x15, other arithmetic, combine(): jnp.exp(later[0])[:, None, None] * earlier[1] + later[1]  30.9 us
    all_gather x1, blocking collectives, carried_in_2(): gathered = jax.tree.map(lambda a: lax.all_gather(a, axis), part)  29 us
  transfers between devices with their start and end apart: 5, of which 4 were waited for; matrix products, arithmetic and copies ran while one was open for 14% of the time, Pallas kernels for 0%

commit v1 on v0

v1 whole, which is shorter than its diff:
```python
import functools

import jax
import jax.numpy as jnp
from jax import lax
from jax.experimental import pallas as pl
from jax.experimental.pallas import tpu as pltpu
from jax.sharding import PartitionSpec as P

RING = 4
NT = (((1,), (1,)), ((), ()))
TN = (((0,), (0,)), ((), ()))
NN = (((1,), (0,)), ((), ()))


def mm(a, b, dims):
    return lax.dot_general(a, b, dims, preferred_element_type=jnp.float32)


def mm_exact(a, b, dims):
    return lax.dot_general(
        a, b, dims, precision=lax.Precision.HIGHEST, preferred_element_type=jnp.float32
    )


def spread(columns, width):
    rows = columns.shape[0]
    return jnp.concatenate(
        [jnp.broadcast_to(columns[:, h : h + 1], (rows, width)) for h in range(columns.shape[1])],
        axis=1,
    )


def own_kernel(heads, x, dy, b, c, cum, cum_t, ends, write_local, read_local, total):
    g = pl.program_id(0)
    rows = x.shape[0]
    half = rows // 2
    width = x.shape[1] // heads

    @pl.when(g == 0)
    def _():
        total[...] = jnp.zeros_like(total)

    col = cum[0]
    mid = col[half - 1 : half, :]
    last = col[rows - 1 : rows, :]
    later = lax.broadcasted_iota(jnp.int32, (half, half), 1) >= lax.broadcasted_iota(
        jnp.int32, (half, half), 0
    )
    for i in range(2):
        lo = i * half
        acc = jnp.zeros((half, half), jnp.float32)
        for h in range(heads):
            span = slice(h * width, (h + 1) * width)
            log = cum_t[0, h : h + 1, lo : lo + half] - col[lo : lo + half, h : h + 1]
            decay = jnp.exp(jnp.where(later, log, -jnp.inf))
            acc += decay * mm(x[lo : lo + half, span], dy[lo : lo + half, span], NT)
        total[lo : lo + half, lo : lo + half] += acc
    xf = x[...].astype(jnp.float32)
    early = (xf[:half] * spread(jnp.exp(mid - col[:half]), width)).astype(jnp.bfloat16)
    late = (
        dy[half:, :].astype(jnp.float32) * spread(jnp.exp(col[half:] - mid), width)
    ).astype(jnp.bfloat16)
    total[:half, half:] += mm(early, late, NT)
    tailed = (xf * spread(jnp.exp(last - col), width)).astype(jnp.bfloat16)
    ends[0] = mm(b[...], tailed, TN).astype(ends.dtype)

    @pl.when(g == pl.num_programs(0) - 1)
    def _():
        write_local[...] = mm_exact(total[...], c[...].astype(jnp.float32), NN)
        read_local[...] = mm_exact(total[...], b[...].astype(jnp.float32), TN)


def front_kernel(heads, top, bottom, c, cum, fronts):
    half = top.shape[0]
    width = top.shape[1] // heads
    decay = jnp.exp(cum[0])
    first = (top[...].astype(jnp.float32) * spread(decay[:half], width)).astype(jnp.bfloat16)
    second = (bottom[...].astype(jnp.float32) * spread(decay[half:], width)).astype(jnp.bfloat16)
    fronts[0] = (mm(c[:half], first, TN) + mm(c[half:], second, TN)).astype(fronts.dtype)


def act_kernel(heads, with_write, coef, top, bottom, b, c, cum, cum_t, *rest):
    if with_write:
        x, *rest = rest
    fronts, (carried, act, *rest) = rest[:RING], rest[RING:]
    g = pl.program_id(0)
    half = top.shape[0]
    rows = 2 * half
    width = top.shape[1] // heads
    col = cum[0]
    mid = col[half - 1 : half, :]
    last = col[rows - 1 : rows, :]
    tail = jnp.exp(last - col)
    later = lax.broadcasted_iota(jnp.int32, (half, half), 1) >= lax.broadcasted_iota(
        jnp.int32, (half, half), 0
    )
    pieces = []
    for h in range(heads):
        span = slice(h * width, (h + 1) * width)
        at = g * heads + h
        piece = carried[0, :, span].astype(jnp.float32) * coef[RING, at]
        for i in range(RING):
            piece += fronts[i][0, :, span].astype(jnp.float32) * coef[i, at]
        pieces.append(piece.astype(jnp.bfloat16))
    grads = jnp.concatenate(pieces, axis=1)
    carry = mm(b[...], grads, NN)
    scores = mm(b[...], c[...], NT)
    late = (
        bottom[...].astype(jnp.float32) * spread(jnp.exp(col[half:] - mid), width)
    ).astype(jnp.bfloat16)
    cross = mm(scores[:half, half:].astype(jnp.bfloat16), late, NN)
    to_mid = jnp.exp(mid - col[:half])
    for i, dy in enumerate((top, bottom)):
        lo = i * half
        score = scores[lo : lo + half, lo : lo + half]
        for h in range(heads):
            span = slice(h * width, (h + 1) * width)
            log = cum_t[0, h : h + 1, lo : lo + half] - col[lo : lo + half, h : h + 1]
            decay = jnp.exp(jnp.where(later, log, -jnp.inf))
            out = mm((decay * score).astype(jnp.bfloat16), dy[:, span], NN)
            out += carry[lo : lo + half, span] * tail[lo : lo + half, h : h + 1]
            if i == 0:
                out += cross[:, span] * to_mid[:, h : h + 1]
            act[lo : lo + half, span] = out.astype(act.dtype)
    if with_write:
        (write,) = rest
        tailed = (x[...].astype(jnp.float32) * spread(tail, width)).astype(jnp.bfloat16)

        @pl.when(g == 0)
        def _():
            write[...] = jnp.zeros_like(write)

        write[...] += mm(tailed, grads, NT)


def read_kernel(heads, quarter, coef, *refs):
    dys, refs = refs[: RING + 1], refs[RING + 1 :]
    cums, refs = refs[:RING], refs[RING:]
    ends, carried, out = refs[:RING], refs[RING], refs[RING + 1]
    rows = out.shape[1]
    width = carried.shape[1] // heads
    for j in range(RING):
        pieces = []
        for h in range(heads):
            span = slice(h * width, (h + 1) * width)
            piece = carried[:, span].astype(jnp.float32) * coef[j * (RING + 1) + RING, h]
            for i in range(RING):
                piece += ends[i][:, span].astype(jnp.float32) * coef[j * (RING + 1) + i, h]
            pieces.append(piece.astype(jnp.bfloat16))
        states = jnp.concatenate(pieces, axis=1)
        decay = spread(jnp.exp(cums[j][0]), width)
        if j < RING - 1:
            dy = (dys[j][...].astype(jnp.float32) * decay).astype(jnp.bfloat16)
            out[j] = mm(dy, states, NT).astype(out.dtype)
        else:
            half = rows // 2
            for i in range(2):
                at = slice(i * half, (i + 1) * half)
                dy = (dys[j + i][...].astype(jnp.float32) * decay[at]).astype(jnp.bfloat16)
                out[j, at] = mm(dy, states, NT).astype(out.dtype)


def product_kernel(*refs):
    acts, (w, out, total) = refs[:RING], refs[RING:]
    k = pl.program_id(0)
    for j in range(RING):
        part = mm(acts[j][...], w[...], NT)

        @pl.when(k == 0)
        def _():
            total[j] = part

        @pl.when(k > 0)
        def _():
            total[j] += part

    @pl.when(k == pl.num_programs(0) - 1)
    def _():
        out[...] = total[...].astype(out.dtype)


def params():
    return pltpu.CompilerParams(vmem_limit_bytes=48 * 2**20)


def cost(flops, size):
    return pl.CostEstimate(flops=int(flops), bytes_accessed=int(size), transcendentals=0)


def whole(shape):
    return pl.BlockSpec(shape, lambda g: (0,) * len(shape))


def local(x, dy, write_proj, read_proj, log_decay, w_in):
    rows, columns = x.shape
    half = rows // 2
    state_dim = write_proj.shape[1]
    n_heads = log_decay.shape[1]
    heads = n_heads // RING
    width = columns // n_heads
    part = heads * width
    n_seq, n_head = lax.axis_size("seq"), lax.axis_size("head")
    outer = n_seq // RING
    place = lax.axis_index("seq")
    p, z = place % RING, place // RING
    bf16, f32 = jnp.bfloat16, jnp.float32

    def swap(value, j):
        return lax.ppermute(value, "seq", [(s, s ^ j) for s in range(n_seq)])

    def along(value, d):
        return lax.ppermute(
            value, "seq", [(s, s + d * RING) for s in range(n_seq) if 0 <= s + d * RING < n_seq]
        )

    logs = [log_decay] + [swap(log_decay, j) for j in range(1, RING)]
    projections = jnp.concatenate([write_proj, read_proj], axis=1)
    projections = [projections] + [swap(projections, j) for j in range(1, RING)]
    dy_x, dy_y = swap(dy, 1), swap(dy, 2)
    dy_top, dy_bottom = swap(dy_x[:half], 2), swap(dy_y[half:], 1)
    turn = [(s, (s + RING) % n_seq) for s in range(n_seq)]
    w_blocks = [w_in]
    for _ in range(outer - 1):
        w_blocks.append(lax.ppermute(w_blocks[-1], "seq", turn))

    writes = [write_proj] + [v[:, :state_dim] for v in projections[1:]]
    reads = [read_proj] + [v[:, state_dim:] for v in projections[1:]]
    cums = jnp.cumsum(jnp.stack(logs), axis=1)
    totals = cums[:, -1, :]
    cum_groups = [cums[j].reshape(rows, RING, heads).swapaxes(0, 1) for j in range(RING)]
    cum_rows = [cums[j].T.reshape(RING, heads, rows) for j in range(RING)]

    order = p ^ jnp.arange(RING)

    def decay_over(mask):
        return jnp.exp(jnp.sum(jnp.where(mask[..., None], totals, 0.0), axis=-2))

    later = order[None, :] > order[:, None]
    between = later[:, None, :] & later.T[None, :, :]
    grad_coef = jnp.where(later[:, :, None], decay_over(between), 0.0)
    grad_coef = jnp.concatenate([grad_coef, decay_over(later)[:, None]], axis=1)
    state_coef = jnp.where(later.T[:, :, None], decay_over(between.swapaxes(0, 1)), 0.0)
    state_coef = jnp.concatenate([state_coef, decay_over(later.T)[:, None]], axis=1)
    front_weight, end_weight = decay_over(later.T), decay_over(later)
    ring_log = jnp.sum(totals, axis=0)

    def my_heads(value):
        return lax.dynamic_slice_in_dim(value, p * heads, heads, value.ndim - 1)

    group = lambda g: (0, g)
    group3 = lambda g: (g, 0, 0)
    by_group = pl.BlockSpec((rows, part), group)
    top_spec = pl.BlockSpec((half, part), group)
    low_spec = pl.BlockSpec((half, part), lambda g: (1, g))
    proj_spec = whole((rows, state_dim))
    cum_spec = pl.BlockSpec((1, rows, heads), group3)
    cum_row_spec = pl.BlockSpec((1, heads, rows), group3)
    state_spec = pl.BlockSpec((1, state_dim, part), group3)
    state_shape = jax.ShapeDtypeStruct((RING, state_dim, part), bf16)
    block_bytes = rows * columns * 2

    ends, write_local, read_local = pl.pallas_call(
        functools.partial(own_kernel, heads),
        grid=(RING,),
        in_specs=[by_group, by_group, proj_spec, proj_spec, cum_spec, cum_row_spec],
        out_specs=[state_spec, proj_spec, proj_spec],
        out_shape=[state_shape] + [jax.ShapeDtypeStruct((rows, state_dim), f32)] * 2,
        scratch_shapes=[pltpu.VMEM((rows, rows), f32)],
        compiler_params=params(),
        cost_estimate=cost(2 * rows * columns * 600, 3 * block_bytes),
        name="own_tokens",
    )(x, dy, write_proj, read_proj, cum_groups[0], cum_rows[0])

    blocks = [(dy, dy), (dy_x, dy_x), (dy_y, dy_y), (dy_top, dy_bottom)]
    specs = [(top_spec, low_spec)] * 3 + [(top_spec, top_spec)]
    fronts = [
        pl.pallas_call(
            functools.partial(front_kernel, heads),
            grid=(RING,),
            in_specs=[*specs[j], proj_spec, cum_spec],
            out_specs=state_spec,
            out_shape=state_shape,
            compiler_params=params(),
            cost_estimate=cost(2 * rows * columns * 128, 2 * block_bytes),
            name="fronts",
        )(*blocks[j], reads[j], cum_groups[j])
        for j in range(RING)
    ]

    def wide(values):
        return jnp.repeat(values, width, axis=-1)

    def scan_along(own, log, way):
        span, span_log = own, log
        result, result_log = None, None
        d = 1
        while d < outer:
            got = along(span.astype(bf16), way * d).astype(f32)
            got_log = along(span_log, way * d)
            if result is None:
                result, result_log = got, got_log
            else:
                result = result + wide(jnp.exp(result_log)) * got
                result_log = result_log + got_log
            span = span + wide(jnp.exp(span_log)) * got
            span_log = span_log + got_log
            d *= 2
        return result.astype(bf16)

    my_log = my_heads(ring_log)[None]
    my_front_weight, my_end_weight = my_heads(front_weight), my_heads(end_weight)

    def mine(value):
        return lax.dynamic_index_in_dim(value, p, 0, False)

    front_sum = sum(
        wide(my_front_weight[j])[None] * mine(fronts[j]).astype(f32) for j in range(RING)
    )
    grad_part = scan_along(front_sum, my_log, -1)
    grad_parts = jnp.stack([grad_part] + [swap(grad_part, j) for j in range(1, RING)])
    grad_in = jnp.take(grad_parts, order, axis=0)

    my_ends = [mine(ends)] + [
        swap(lax.dynamic_index_in_dim(ends, p ^ j, 0, False), j) for j in range(1, RING)
    ]
    end_sum = sum(wide(my_end_weight[j])[None] * my_ends[j].astype(f32) for j in range(RING))
    state_part = scan_along(end_sum, my_log, 1)

    acts = []
    for j in range(RING):
        extra = j == 0
        out = pl.pallas_call(
            functools.partial(act_kernel, heads, extra),
            grid=(RING,),
            in_specs=[pl.BlockSpec(memory_space=pltpu.SMEM)]
            + [*specs[j], proj_spec, proj_spec, cum_spec, cum_row_spec]
            + [by_group] * extra
            + [state_spec] * (RING + 1),
            out_specs=[by_group] + [proj_spec] * extra,
            out_shape=[jax.ShapeDtypeStruct((rows, columns), bf16)]
            + [jax.ShapeDtypeStruct((rows, state_dim), f32)] * extra,
            compiler_params=params(),
            cost_estimate=cost(2 * rows * columns * 600, 5 * block_bytes),
            name="act_grad",
        )(
            grad_coef[j],
            *blocks[j],
            writes[j],
            reads[j],
            cum_groups[j],
            cum_rows[j],
            *([x] * extra),
            *fronts,
            grad_in,
        )
        acts.append(out[0])
        if extra:
            write_carry = out[1]
    act_grad = acts[0]

    pick = lambda g, q: (0, q[0])
    pick3 = lambda g, q: (q[0], 0, 0)
    fixed2 = lambda g, q: (0, 0)
    read_parts = pl.pallas_call(
        functools.partial(read_kernel, heads),
        grid_spec=pltpu.PrefetchScalarGridSpec(
            num_scalar_prefetch=1,
            grid=(1,),
            in_specs=[pl.BlockSpec(memory_space=pltpu.SMEM)]
            + [pl.BlockSpec((rows, part), pick)] * 3
            + [pl.BlockSpec((half, part), pick)] * 2
            + [pl.BlockSpec((1, rows, heads), pick3)] * RING
            + [pl.BlockSpec((state_dim, part), fixed2)] * (RING + 1),
            out_specs=pl.BlockSpec((RING, rows, state_dim), lambda g, q: (0, 0, 0)),
        ),
        out_shape=jax.ShapeDtypeStruct((RING, rows, state_dim), bf16),
        compiler_params=params(),
        cost_estimate=cost(2 * rows * columns * 128, 2 * block_bytes),
        name="read_carry",
    )(
        p.astype(jnp.int32)[None],
        my_heads(state_coef).reshape(RING * (RING + 1), heads),
        dy,
        dy_x,
        dy_y,
        dy_top,
        dy_bottom,
        *cum_groups,
        *my_ends,
        state_part,
    )
    read_carry = read_parts[0].astype(f32) + sum(
        swap(read_parts[j], j).astype(f32) for j in range(1, RING)
    )

    both = jnp.stack([write_local + write_carry, read_local + read_carry])
    if n_head == 2:
        both = both + lax.ppermute(both, "head", [(0, 1), (1, 0)])
    else:
        both = lax.psum(both, "head")

    depth = min(512, columns)
    w_rows = w_in.shape[0]
    tiles = [
        pl.pallas_call(
            product_kernel,
            grid=(columns // depth,),
            in_specs=[pl.BlockSpec((rows, depth), group)] * RING
            + [pl.BlockSpec((w_rows, depth), group)],
            out_specs=whole((RING, rows, w_rows)),
            out_shape=jax.ShapeDtypeStruct((RING, rows, w_rows), bf16),
            scratch_shapes=[pltpu.VMEM((RING, rows, w_rows), f32)],
            compiler_params=params(),
            cost_estimate=cost(2 * RING * rows * columns * w_rows, 5 * block_bytes),
            name="product",
        )(*acts, w)
        for w in w_blocks
    ]
    tiles = jnp.stack(tiles)
    share = outer // n_head
    side = lax.axis_index("head")
    if n_head == 2:
        def of(h):
            return jnp.take(tiles, (z - (h * share + jnp.arange(share))) % outer, axis=0)

        got = lax.ppermute(of(1 - side), "head", [(0, 1), (1, 0)])
        summed = (of(side).astype(f32) + got.astype(f32)).astype(bf16)
    else:
        tiles = jnp.take(tiles, (z - jnp.arange(outer)) % outer, axis=0)
        summed = lax.psum_scatter(tiles, "head", scatter_dimension=0, tiled=True)
    columns_of = jnp.stack([summed[:, 0]] + [swap(summed[:, j], j) for j in range(1, RING)])
    columns_of = jnp.take(columns_of, order, axis=0)
    input_grad = columns_of.transpose(2, 1, 0, 3).reshape(rows, share * RING * w_rows)
    return (input_grad, act_grad, both[0], both[1])


def solution(mesh):
    return jax.shard_map(
        local,
        mesh=mesh,
        in_specs=(
            P("seq", "head"),
            P("seq", "head"),
            P("seq", None),
            P("seq", None),
            P("seq", "head"),
            P("seq", "head"),
        ),
        out_specs=(P("seq", "head"), P("seq", "head"), P("seq", None), P("seq", None)),
        check_vma=False,
    )
```

time: 972 us -> 325 us (0.33)
  waiting for transfers between devices: 728 us -> 125 us
  Pallas kernels: 0 us -> 104 us
  matrix products: 64.7 us -> 0 us
  blocking collectives: 63.8 us -> 0 us
  other arithmetic: 75.7 us -> 18.9 us
  starting transfers between devices: 0.2 us -> 41.5 us
  between operations: 14 us -> 1.77 us
    all_gather x3 -> x0, waiting for transfers between devices: 718 us -> none  [the longest x1 306 us: carried_in_2(): gathered = jax.tree.map(lambda a: lax.all_gather(a, axis), part)]
    ppermute x0 -> x33, waiting for transfers between devices: none -> 125 us  [the longest x6 71.1 us: along(): lax.ppermute(value, 'seq', [(s, s + d * RING) for s in range(n_seq) if 0...]
    pallas_call x0 -> x14, Pallas kernels: none -> 104 us  [the longest x4 49.7 us: local(): pl.pallas_call(product_kernel, grid=(columns // depth,), in_specs=[pl.Blo...]
    dot_general x11 -> x0, matrix products: 64.7 us -> none  [the longest x1 16.9 us: local(): lax.dot_general(act_grad, lax.all_gather(w_in, 'seq', axis=0, tiled=True)...]
    all_gather x2 -> x0, blocking collectives: 63.8 us -> none  [the longest x1 34.8 us: carried_in(): lax.all_gather(part.astype(kind), axis)]
    ppermute x0 -> x33, starting transfers between devices: none -> 41.5 us  [the longest x22 21.8 us: swap(): return lax.ppermute(value, 'seq', [(s, s ^ j) for s in range(n_seq)])]
    select_n x16 -> x4, other arithmetic: 36 us -> 4.16 us  [the longest x1 2.49 us: of(): jnp.take(tiles, (z - (h * share + jnp.arange(share))) % outer, axis=0)]
    add x15 -> x1, other arithmetic: 30.9 us -> 0.03 us  [local(): both = both + lax.ppermute(both, 'head', [(0, 1), (1, 0)])]
  transfers between devices with their start and end apart: 5 -> 33, of which waited for: 4 -> 15; matrix products, arithmetic and copies ran while one was open for 14% -> 13% of each run, Pallas kernels for 0% -> 32%
where the time goes in v1:
time: 325 us; the launch traced here: 322 us
  waiting for transfers between devices  125 us (38%)
  Pallas kernels  104 us (32%)
  starting transfers between devices  41.5 us (13%)
  local copies, waits for them, and re-layouts  31.1 us (10%)
  other arithmetic  18.9 us (6%)
    ppermute x6, waiting for transfers between devices, along(): lax.ppermute(value, 'seq', [(s, s + d * RING) for s in range(n_seq) if 0...  71.1 us
    ppermute x22, waiting for transfers between devices, swap(): return lax.ppermute(value, 'seq', [(s, s ^ j) for s in range(n_seq)])  51.9 us
    pallas_call x4, Pallas kernels, local(): pl.pallas_call(product_kernel, grid=(columns // depth,), in_specs=[pl.Blo...  49.7 us
    pallas_call x4, Pallas kernels, local(): pl.pallas_call(functools.partial(act_kernel, heads, extra), grid=(RING,),...  29.7 us
    ppermute x22, starting transfers between devices, swap(): return lax.ppermute(value, 'seq', [(s, s ^ j) for s in range(n_seq)])  21.8 us
    pallas_call x4, Pallas kernels, local(): pl.pallas_call(functools.partial(front_kernel, heads), grid=(RING,), in_s...  15 us
    ppermute x6, starting transfers between devices, along(): lax.ppermute(value, 'seq', [(s, s + d * RING) for s in range(n_seq) if 0...  11.2 us
    unnamed x142, local copies, waits for them, and re-layouts  6.75 us
  transfers between devices with their start and end apart: 33, of which 15 were waited for; matrix products, arithmetic and copies ran while one was open for 13% of the time, Pallas kernels for 32%

profile of v1, /device:TPU:1, one launch (start us, length us, event | category | flops | bytes accessed | tf_op | source)
XLA Modules:
  0.0 322.4 jit_solution(14510732375755268972)
XLA Ops:
  0.6 2.1 collective-permute-start
  14.7 2.3 reduce-window.6
  20.2 3.7 %collective-permute-start.27 = (f32[1,8]{1,0:T(1,128)}, f32[1,8]{1,0:T(1,128)}, u32[]{:S(2)}, u32[]{:S(2)}) collective-permute-start(f32[1,8]{1,0:T(1,128)} %get-tuple-element.81), channel_id=1, source_target_pairs={{0,8},{2,10},{4,12},{6,14},{8,16},{10,18},{12,20},{14,22},{16,24},... | collective-permute-start | bytes 104 | tf_op jit(solution)/shard_map/ppermute | solution.py:213
  26.2 3.0 fronts.4.rest_1_.rest_0_
  29.3 6.3 %own_tokens.1 = (bf16[4,128,1024]{2,1,0:T(8,128)(2,1)S(1)}, f32[256,128]{1,0:T(8,128)S(1)}, f32[256,128]{1,0:T(8,128)S(1)}) custom-call(bf16[256,4096]{1,0:T(8,128)(2,1)S(1)} %copy-done.31, bf16[256,4096]{1,0:T(8,128)(2,1)S(1)} %copy-done, bf16[256,128]{1,0:T(8,128)(2,1)S(1)} %copy-done.39, bf16[256,128]{1,0:T(8,128)(2,1)S(1)} %copy-done.38, ...), custom_call_target="tpu_custom_call" | custom-call | flops 1258291200 | bytes 6291456 | tf_op jit(solution)/shard_map/own_tokens/pallas_call | solution.py:263
  36.2 14.6 %collective-permute-done.3.top.bottom.refs_1_ = bf16[256,4096]{1,0:T(8,128)(2,1)} collective-permute-done((bf16[256,4096]{1,0:T(8,128)(2,1)}, bf16[256,4096]{1,0:T(8,128)(2,1)}, u32[]{:S(2)}, u32[]{:S(2)}) %collective-permute-start.3) | collective-permute-done | bytes 2097184 | tf_op jit(solution)/shard_map/ppermute | solution.py:210
  58.1 1.8 collective-permute-done.16.refs_4_
  63.7 14.9 %collective-permute-done.4 = bf16[256,256]{1,0:T(8,128)(2,1)S(1)} collective-permute-done((bf16[256,256]{1,0:T(8,128)(2,1)}, bf16[256,256]{1,0:T(8,128)(2,1)S(1)}, u32[]{:S(2)}, u32[]{:S(2)}) %collective-permute-start.4) | collective-permute-done | bytes 131104 | tf_op jit(solution)/shard_map/ppermute | solution.py:210
  82.4 4.3 %fronts.5.rest_2_.rest_1_ = bf16[4,128,1024]{2,1,0:T(8,128)(2,1)S(1)} custom-call(bf16[256,4096]{1,0:T(8,128)(2,1)} %collective-permute-done.3.top.bottom.refs_1_, bf16[256,4096]{1,0:T(8,128)(2,1)} %collective-permute-done.3.top.bottom.refs_1_, bf16[256,128]{1,0:T(8,128)(2,1)S(1)} %get-tuple-element.64.c, f32[4,256,8]{2,1,0:T(8,128)S(1)} %bitcast.205), custom_call_target="tpu_custom_call" | custom-call | flops 268435456 | bytes 4194304 | tf_op jit(solution)/shard_map/fronts/pallas_call | solution.py:278
  86.8 4.6 %fronts.6.rest_3_.rest_2_ = bf16[4,128,1024]{2,1,0:T(8,128)(2,1)S(1)} custom-call(bf16[256,4096]{1,0:T(8,128)(2,1)} %collective-permute-done.5.top.bottom.refs_2_, bf16[256,4096]{1,0:T(8,128)(2,1)} %collective-permute-done.5.top.bottom.refs_2_, bf16[256,128]{1,0:T(8,128)(2,1)S(1)} %get-tuple-element.62.c, f32[4,256,8]{2,1,0:T(8,128)S(1)} %bitcast.208), custom_call_target="tpu_custom_call" | custom-call | flops 268435456 | bytes 4194304 | tf_op jit(solution)/shard_map/fronts/pallas_call | solution.py:278
  91.6 3.0 fronts.7.rest_4_.rest_3_
  98.2 16.9 %collective-permute-done.10 = bf16[128,1024]{1,0:T(8,128)(2,1)S(1)} collective-permute-done((bf16[128,1024]{1,0:T(8,128)(2,1)S(1)}, bf16[128,1024]{1,0:T(8,128)(2,1)S(1)}, u32[]{:S(2)}, u32[]{:S(2)}) %collective-permute-start.10) | collective-permute-done | bytes 262176 | tf_op jit(solution)/shard_map/ppermute | solution.py:213
  118.6 3.6 %collective-permute-start.18 = (bf16[256,4096]{1,0:T(8,128)(2,1)}, bf16[256,4096]{1,0:T(8,128)(2,1)}, u32[]{:S(2)}, u32[]{:S(2)}) collective-permute-start(bf16[256,4096]{1,0:T(8,128)(2,1)} %collective-permute-done.17.refs_4_), channel_id=1, source_target_pairs={{0,8},{2,10},{4,12},{6,14},{8,16},{10,18},{12,20},{14,22},{16,24},... | collective-permute-start | bytes 6291464 | tf_op jit(solution)/shard_map/ppermute | solution.py:225
  122.2 54.1 %collective-permute-done.12 = bf16[128,1024]{1,0:T(8,128)(2,1)S(1)} collective-permute-done((bf16[128,1024]{1,0:T(8,128)(2,1)S(1)}, bf16[128,1024]{1,0:T(8,128)(2,1)S(1)}, u32[]{:S(2)}, u32[]{:S(2)}) %collective-permute-start.12) | collective-permute-done | bytes 262176 | tf_op jit(solution)/shard_map/ppermute | solution.py:213
  180.1 2.0 collective-permute-start.28
  182.1 1.8 collective-permute-done.13
  184.6 5.9 %collective-permute-done.15 = bf16[128,1024]{1,0:T(8,128)(2,1)S(1)} collective-permute-done((bf16[128,1024]{1,0:T(8,128)(2,1)S(1)}, bf16[128,1024]{1,0:T(8,128)(2,1)S(1)}, u32[]{:S(2)}, u32[]{:S(2)}) %collective-permute-start.15) | collective-permute-done | bytes 262176 | tf_op jit(solution)/shard_map/ppermute | solution.py:210
  191.7 3.0 gather_fusion
  196.4 8.4 %act_grad.4 = (bf16[256,4096]{1,0:T(8,128)(2,1)}, f32[256,128]{1,0:T(8,128)S(1)}) custom-call(f32[5,32]{1,0:T(8,128)S(1)} %copy-done.62, bf16[256,4096]{1,0:T(8,128)(2,1)} %refs_0_.1, bf16[256,4096]{1,0:T(8,128)(2,1)} %refs_0_.1, bf16[256,128]{1,0:T(8,128)(2,1)S(1)} %copy-done.39, bf16[256,128]{1,0:T(8,128)(2,1)S(1)} %copy-done.38, ...), custom_call_target="tpu_custom_call" | custom-call | flops 1258291200 | bytes 10485760 | tf_op jit(solution)/shard_map/act_grad/pallas_call | solution.py:333
  205.6 7.2 %act_grad.7.refs_3_ = bf16[256,4096]{1,0:T(8,128)(2,1)} custom-call(f32[5,32]{1,0:T(8,128)S(1)} %copy-done.61, bf16[128,4096]{1,0:T(8,128)(2,1)S(1)} %copy-done.18, bf16[128,4096]{1,0:T(8,128)(2,1)S(1)} %copy-done.21, bf16[256,128]{1,0:T(8,128)(2,1)S(1)} %copy-done.49, bf16[256,128]{1,0:T(8,128)(2,1)S(1)} %copy-done.43, f32[4,256,8]{2,1,0:T(8,128)S(1)} %bitcast.212, ...), custom_call_target="tpu_custom_call" | custom-call | flops 1258291200 | bytes 10485760 | tf_op jit(solution)/shard_map/act_grad/pallas_call | solution.py:333
  213.0 7.0 %act_grad.6.refs_2_ = bf16[256,4096]{1,0:T(8,128)(2,1)} custom-call(f32[5,32]{1,0:T(8,128)S(1)} %copy-done.60, bf16[256,4096]{1,0:T(8,128)(2,1)} %collective-permute-done.5.top.bottom.refs_2_, bf16[256,4096]{1,0:T(8,128)(2,1)} %collective-permute-done.5.top.bottom.refs_2_, bf16[256,128]{1,0:T(8,128)(2,1)S(1)} %copy-done.50, bf16[256,128]{1,0:T(8,128)(2,1)S(1)} %copy-done.45, ...), custom_call_target="tpu_custom_call" | custom-call | flops 1258291200 | bytes 10485760 | tf_op jit(solution)/shard_map/act_grad/pallas_call | solution.py:333
  221.3 7.0 %act_grad.5.refs_1_ = bf16[256,4096]{1,0:T(8,128)(2,1)} custom-call(f32[5,32]{1,0:T(8,128)S(1)} %get-tuple-element.67.coef, bf16[256,4096]{1,0:T(8,128)(2,1)} %collective-permute-done.3.top.bottom.refs_1_, bf16[256,4096]{1,0:T(8,128)(2,1)} %collective-permute-done.3.top.bottom.refs_1_, bf16[256,128]{1,0:T(8,128)(2,1)S(1)} %copy-done.48, ...), custom_call_target="tpu_custom_call" | custom-call | flops 1258291200 | bytes 10485760 | tf_op jit(solution)/shard_map/act_grad/pallas_call | solution.py:333
  229.9 12.3 %product.4 = bf16[4,256,256]{2,1,0:T(8,128)(2,1)S(1)} custom-call(bf16[256,4096]{1,0:T(8,128)(2,1)S(1)} %copy-done.2, bf16[256,4096]{1,0:T(8,128)(2,1)S(1)} %copy-done.1, bf16[256,4096]{1,0:T(8,128)(2,1)} %act_grad.6.refs_2_, bf16[256,4096]{1,0:T(8,128)(2,1)} %act_grad.7.refs_3_, bf16[256,4096]{1,0:T(8,128)(2,1)} %refs_4_.1), custom_call_target="tpu_custom_call" | custom-call | flops 2147483648 | bytes 10485760 | tf_op jit(solution)/shard_map/product/pallas_call | solution.py:406
  242.2 12.4 %product.5 = bf16[4,256,256]{2,1,0:T(8,128)(2,1)S(1)} custom-call(bf16[256,4096]{1,0:T(8,128)(2,1)S(1)} %copy-done.2, bf16[256,4096]{1,0:T(8,128)(2,1)S(1)} %copy-done.1, bf16[256,4096]{1,0:T(8,128)(2,1)} %act_grad.6.refs_2_, bf16[256,4096]{1,0:T(8,128)(2,1)} %act_grad.7.refs_3_, bf16[256,4096]{1,0:T(8,128)(2,1)} %collective-permute-done.16.refs_4_), custom_call_target="tpu_custom_call" | custom-call | flops 2147483648 | bytes 10485760 | tf_op jit(solution)/shard_map/product/pallas_call | solution.py:406
  254.6 12.4 %product.6 = bf16[4,256,256]{2,1,0:T(8,128)(2,1)S(1)} custom-call(bf16[256,4096]{1,0:T(8,128)(2,1)S(1)} %copy-done.2, bf16[256,4096]{1,0:T(8,128)(2,1)S(1)} %copy-done.1, bf16[256,4096]{1,0:T(8,128)(2,1)} %act_grad.6.refs_2_, bf16[256,4096]{1,0:T(8,128)(2,1)} %act_grad.7.refs_3_, bf16[256,4096]{1,0:T(8,128)(2,1)} %collective-permute-done.17.refs_4_), custom_call_target="tpu_custom_call" | custom-call | flops 2147483648 | bytes 10485760 | tf_op jit(solution)/shard_map/product/pallas_call | solution.py:406
  267.0 12.6 %product.7 = bf16[4,256,256]{2,1,0:T(8,128)(2,1)S(1)} custom-call(bf16[256,4096]{1,0:T(8,128)(2,1)S(1)} %copy-done.2, bf16[256,4096]{1,0:T(8,128)(2,1)S(1)} %copy-done.1, bf16[256,4096]{1,0:T(8,128)(2,1)} %act_grad.6.refs_2_, bf16[256,4096]{1,0:T(8,128)(2,1)} %act_grad.7.refs_3_, bf16[256,4096]{1,0:T(8,128)(2,1)} %collective-permute-done.18.refs_4_), custom_call_target="tpu_custom_call" | custom-call | flops 2147483648 | bytes 10485760 | tf_op jit(solution)/shard_map/product/pallas_call | solution.py:406
  281.2 3.4 %gather_fusion.3 = bf16[2,4,256,256]{3,2,1,0:T(8,128)(2,1)} fusion(bf16[4,4,256,256]{3,2,1,0:T(8,128)(2,1)} %pad_maximum_fusion, s32[1024]{0:T(1024)} %pad_clamp_fusion), kind=kCustom, calls=%fused_computation.1.clone | custom fusion | bytes 2097160 | tf_op jit(solution)/shard_map/jit(_take)/gather | solution.py:425
  284.7 2.5 broadcast_select_fusion
  289.8 3.6 %read_carry.1 = bf16[4,256,128]{2,1,0:T(8,128)(2,1)S(1)} custom-call(s32[1]{0:T(128)} %bitcast.70.quarter, f32[20,8]{1,0:T(8,128)S(1)} %reshape.275.coef, bf16[256,4096]{1,0:T(8,128)(2,1)} %refs_0_.1, bf16[256,4096]{1,0:T(8,128)(2,1)} %collective-permute-done.3.top.bottom.refs_1_, bf16[256,4096]{1,0:T(8,128)(2,1)} %collective-permute-done.5.top.bottom.refs_2_, ...), custom_call_target="tpu_custom_call" | custom-call | flops 268435456 | bytes 4194304 | tf_op jit(solution)/shard_map/read_carry/pallas_call | solution.py:365
  300.9 2.2 gather_fusion.2
  308.4 4.5 %collective-permute-done.20 = bf16[2,256,256]{2,1,0:T(8,128)(2,1)S(1)} collective-permute-done((bf16[2,256,256]{2,1,0:T(8,128)(2,1)S(1)}, bf16[2,256,256]{2,1,0:T(8,128)(2,1)S(1)}, u32[]{:S(2)}, u32[]{:S(2)}) %collective-permute-start.20) | collective-permute-done | bytes 262176 | tf_op jit(solution)/shard_map/ppermute | solution.py:210
  314.2 5.1 %collective-permute-done.22 = bf16[2,256,256]{2,1,0:T(8,128)(2,1)S(1)} collective-permute-done((bf16[2,256,256]{2,1,0:T(8,128)(2,1)S(1)}, bf16[2,256,256]{2,1,0:T(8,128)(2,1)S(1)}, u32[]{:S(2)}, u32[]{:S(2)}) %collective-permute-start.22) | collective-permute-done | bytes 262176 | tf_op jit(solution)/shard_map/ppermute | solution.py:210
  (270 shorter events, 71.9 us)
Async XLA Ops:
  0.6 11.8 %collective-permute-start = (f32[256,32]{0,1:T(8,128)}, f32[256,32]{0,1:T(8,128)S(1)}, u32[]{:S(2)}, u32[]{:S(2)}) collective-permute-start(f32[256,32]{0,1:T(8,128)} %param.12), channel_id=1, source_target_pairs={{0,2},{2,0},{4,6},{6,4},{8,10},{10,8},{12,14},{14,12},{16,18},{18,... | collective-permute-start | bytes 98312 | tf_op jit(solution)/shard_map/ppermute | solution.py:210
  2.7 9.8 %collective-permute-start.1 = (f32[256,32]{0,1:T(8,128)}, f32[256,32]{0,1:T(8,128)S(1)}, u32[]{:S(2)}, u32[]{:S(2)}) collective-permute-start(f32[256,32]{0,1:T(8,128)} %param.12), channel_id=1, source_target_pairs={{0,4},{2,6},{4,0},{6,2},{8,12},{10,14},{12,8},{14,10},{16,20},{18,... | collective-permute-start | bytes 98312 | tf_op jit(solution)/shard_map/ppermute | solution.py:210
  4.0 10.0 %collective-permute-start.2 = (f32[256,32]{0,1:T(8,128)}, f32[256,32]{0,1:T(8,128)S(1)}, u32[]{:S(2)}, u32[]{:S(2)}) collective-permute-start(f32[256,32]{0,1:T(8,128)} %param.12), channel_id=1, source_target_pairs={{0,6},{2,4},{4,2},{6,0},{8,14},{10,12},{12,10},{14,8},{16,22},{18,... | collective-permute-start | bytes 98312 | tf_op jit(solution)/shard_map/ppermute | solution.py:210
  4.0 46.8 %collective-permute-start.3 = (bf16[256,4096]{1,0:T(8,128)(2,1)}, bf16[256,4096]{1,0:T(8,128)(2,1)}, u32[]{:S(2)}, u32[]{:S(2)}) collective-permute-start(bf16[256,4096]{1,0:T(8,128)(2,1)} %refs_0_.1), channel_id=1, source_target_pairs={{0,2},{2,0},{4,6},{6,4},{8,10},{10,8},{12,14},{14,12},{16,18},{18,... | collective-permute-start | bytes 6291464 | tf_op jit(solution)/shard_map/ppermute | solution.py:210
  5.4 48.1 %collective-permute-start.5 = (bf16[256,4096]{1,0:T(8,128)(2,1)}, bf16[256,4096]{1,0:T(8,128)(2,1)}, u32[]{:S(2)}, u32[]{:S(2)}) collective-permute-start(bf16[256,4096]{1,0:T(8,128)(2,1)} %refs_0_.1), channel_id=1, source_target_pairs={{0,4},{2,6},{4,0},{6,2},{8,12},{10,14},{12,8},{14,10},{16,20},{18,... | collective-permute-start | bytes 6291464 | tf_op jit(solution)/shard_map/ppermute | solution.py:210
  12.5 48.4 %collective-permute-start.9 = (bf16[256,256]{1,0:T(8,128)(2,1)}, bf16[256,256]{1,0:T(8,128)(2,1)}, u32[]{:S(2)}, u32[]{:S(2)}) collective-permute-start(bf16[256,256]{1,0:T(8,128)(2,1)} %constant_dynamic-update-slice_fusion), channel_id=1, source_target_pairs={{0,6},{2,4},{4,2},{6,0},{8,14},{10,12},{12,10},{14,8},{16,22},{18,... | collective-permute-start | bytes 393224 | tf_op jit(solution)/shard_map/ppermute | solution.py:210
  12.5 47.4 %collective-permute-start.16 = (bf16[256,4096]{1,0:T(8,128)(2,1)}, bf16[256,4096]{1,0:T(8,128)(2,1)}, u32[]{:S(2)}, u32[]{:S(2)}) collective-permute-start(bf16[256,4096]{1,0:T(8,128)(2,1)} %refs_4_.1), channel_id=1, source_target_pairs={{0,8},{2,10},{4,12},{6,14},{8,16},{10,18},{12,20},{14,22},{16,24},... | collective-permute-start | bytes 6291464 | tf_op jit(solution)/shard_map/ppermute | solution.py:225
  20.2 36.7 %collective-permute-start.27 = (f32[1,8]{1,0:T(1,128)}, f32[1,8]{1,0:T(1,128)}, u32[]{:S(2)}, u32[]{:S(2)}) collective-permute-start(f32[1,8]{1,0:T(1,128)} %get-tuple-element.81), channel_id=1, source_target_pairs={{0,8},{2,10},{4,12},{6,14},{8,16},{10,18},{12,20},{14,22},{16,24},... | collective-permute-start | bytes 104 | tf_op jit(solution)/shard_map/ppermute | solution.py:213
  52.1 39.3 %collective-permute-start.7 = (bf16[128,4096]{1,0:T(8,128)(2,1)S(1)}, bf16[128,4096]{1,0:T(8,128)(2,1)S(1)}, u32[]{:S(2)}, u32[]{:S(2)}) collective-permute-start(bf16[128,4096]{1,0:T(8,128)(2,1)S(1)} %slice.170), channel_id=1, source_target_pairs={{0,4},{2,6},{4,0},{6,2},{8,12},{10,14},{12,8},{14,10},{16,20},{18,... | collective-permute-start | bytes 3145736 | tf_op jit(solution)/shard_map/ppermute | solution.py:210
  54.8 36.8 %collective-permute-start.8 = (bf16[128,4096]{1,0:T(8,128)(2,1)S(1)}, bf16[128,4096]{1,0:T(8,128)(2,1)S(1)}, u32[]{:S(2)}, u32[]{:S(2)}) collective-permute-start(bf16[128,4096]{1,0:T(8,128)(2,1)S(1)} %slice.171), channel_id=1, source_target_pairs={{0,2},{2,0},{4,6},{6,4},{8,10},{10,8},{12,14},{14,12},{16,18},{18,... | collective-permute-start | bytes 3145736 | tf_op jit(solution)/shard_map/ppermute | solution.py:210
  56.9 21.7 %collective-permute-start.4 = (bf16[256,256]{1,0:T(8,128)(2,1)}, bf16[256,256]{1,0:T(8,128)(2,1)S(1)}, u32[]{:S(2)}, u32[]{:S(2)}) collective-permute-start(bf16[256,256]{1,0:T(8,128)(2,1)} %constant_dynamic-update-slice_fusion), channel_id=1, source_target_pairs={{0,2},{2,0},{4,6},{6,4},{8,10},{10,8},{12,14},{14,12},{16,18},{18,... | collective-permute-start | bytes 393224 | tf_op jit(solution)/shard_map/ppermute | solution.py:210
  59.9 58.7 %collective-permute-start.17 = (bf16[256,4096]{1,0:T(8,128)(2,1)}, bf16[256,4096]{1,0:T(8,128)(2,1)}, u32[]{:S(2)}, u32[]{:S(2)}) collective-permute-start(bf16[256,4096]{1,0:T(8,128)(2,1)} %collective-permute-done.16.refs_4_), channel_id=1, source_target_pairs={{0,8},{2,10},{4,12},{6,14},{8,16},{10,18},{12,20},{14,22},{16,24},... | collective-permute-start | bytes 6291464 | tf_op jit(solution)/shard_map/ppermute | solution.py:225
  60.9 19.6 %collective-permute-start.6 = (bf16[256,256]{1,0:T(8,128)(2,1)}, bf16[256,256]{1,0:T(8,128)(2,1)S(1)}, u32[]{:S(2)}, u32[]{:S(2)}) collective-permute-start(bf16[256,256]{1,0:T(8,128)(2,1)} %constant_dynamic-update-slice_fusion), channel_id=1, source_target_pairs={{0,4},{2,6},{4,0},{6,2},{8,12},{10,14},{12,8},{14,10},{16,20},{18,... | collective-permute-start | bytes 393224 | tf_op jit(solution)/shard_map/ppermute | solution.py:210
  78.6 18.2 %collective-permute-start.11 = (f32[1,8]{1,0:T(1,128)}, f32[1,8]{1,0:T(1,128)S(1)}, u32[]{:S(2)}, u32[]{:S(2)}) collective-permute-start(f32[1,8]{1,0:T(1,128)} %get-tuple-element.81), channel_id=1, source_target_pairs={{8,0},{10,2},{12,4},{14,6},{16,8},{18,10},{20,12},{22,14},{24,16},... | collective-permute-start | bytes 104 | tf_op jit(solution)/shard_map/ppermute | solution.py:213
  80.5 36.1 %collective-permute-start.23 = (bf16[128,1024]{1,0:T(8,128)(2,1)S(1)}, bf16[128,1024]{1,0:T(8,128)(2,1)S(1)}, u32[]{:S(2)}, u32[]{:S(2)}) collective-permute-start(bf16[128,1024]{1,0:T(8,128)(2,1)S(1)} %get-tuple-element.39), channel_id=1, source_target_pairs={{0,2},{2,0},{4,6},{6,4},{8,10},{10,8},{12,14},{14,12},{16,18},{18,... | collective-permute-start | bytes 786440 | tf_op jit(solution)/shard_map/ppermute | solution.py:210
  91.5 25.2 %collective-permute-start.24 = (bf16[128,1024]{1,0:T(8,128)(2,1)S(1)}, bf16[128,1024]{1,0:T(8,128)(2,1)S(1)}, u32[]{:S(2)}, u32[]{:S(2)}) collective-permute-start(bf16[128,1024]{1,0:T(8,128)(2,1)S(1)} %get-tuple-element.41), channel_id=1, source_target_pairs={{0,4},{2,6},{4,0},{6,2},{8,12},{10,14},{12,8},{14,10},{16,20},{18,... | collective-permute-start | bytes 786440 | tf_op jit(solution)/shard_map/ppermute | solution.py:210
  94.9 20.2 %collective-permute-start.10 = (bf16[128,1024]{1,0:T(8,128)(2,1)S(1)}, bf16[128,1024]{1,0:T(8,128)(2,1)S(1)}, u32[]{:S(2)}, u32[]{:S(2)}) collective-permute-start(bf16[128,1024]{1,0:T(8,128)(2,1)S(1)} %fusion.25), channel_id=1, source_target_pairs={{8,0},{10,2},{12,4},{14,6},{16,8},{18,10},{20,12},{22,14},{24,16},... | collective-permute-start | bytes 786440 | tf_op jit(solution)/shard_map/ppermute | solution.py:213
  96.8 19.8 %collective-permute-start.25 = (bf16[128,1024]{1,0:T(8,128)(2,1)S(1)}, bf16[128,1024]{1,0:T(8,128)(2,1)S(1)}, u32[]{:S(2)}, u32[]{:S(2)}) collective-permute-start(bf16[128,1024]{1,0:T(8,128)(2,1)S(1)} %get-tuple-element.40), channel_id=1, source_target_pairs={{0,6},{2,4},{4,2},{6,0},{8,14},{10,12},{12,10},{14,8},{16,22},{18,... | collective-permute-start | bytes 786440 | tf_op jit(solution)/shard_map/ppermute | solution.py:210
  115.3 61.0 %collective-permute-start.12 = (bf16[128,1024]{1,0:T(8,128)(2,1)S(1)}, bf16[128,1024]{1,0:T(8,128)(2,1)S(1)}, u32[]{:S(2)}, u32[]{:S(2)}) collective-permute-start(bf16[128,1024]{1,0:T(8,128)(2,1)S(1)} %fusion.1), channel_id=1, source_target_pairs={{16,0},{18,2},{20,4},{22,6},{24,8},{26,10},{28,12},{30,14},{17,1},... | collective-permute-start | bytes 786440 | tf_op jit(solution)/shard_map/ppermute | solution.py:213
  116.9 62.2 %collective-permute-start.26 = (bf16[128,1024]{1,0:T(8,128)(2,1)S(1)}, bf16[128,1024]{1,0:T(8,128)(2,1)S(1)}, u32[]{:S(2)}, u32[]{:S(2)}) collective-permute-start(bf16[128,1024]{1,0:T(8,128)(2,1)S(1)} %get-tuple-element.33), channel_id=1, source_target_pairs={{0,8},{2,10},{4,12},{6,14},{8,16},{10,18},{12,20},{14,22},{16,24},... | collective-permute-start | bytes 786440 | tf_op jit(solution)/shard_map/ppermute | solution.py:213
  118.6 148.4 %collective-permute-start.18 = (bf16[256,4096]{1,0:T(8,128)(2,1)}, bf16[256,4096]{1,0:T(8,128)(2,1)}, u32[]{:S(2)}, u32[]{:S(2)}) collective-permute-start(bf16[256,4096]{1,0:T(8,128)(2,1)} %collective-permute-done.17.refs_4_), channel_id=1, source_target_pairs={{0,8},{2,10},{4,12},{6,14},{8,16},{10,18},{12,20},{14,22},{16,24},... | collective-permute-start | bytes 6291464 | tf_op jit(solution)/shard_map/ppermute | solution.py:225
  176.4 7.4 %collective-permute-start.13 = (bf16[128,1024]{1,0:T(8,128)(2,1)S(1)}, bf16[128,1024]{1,0:T(8,128)(2,1)S(1)}, u32[]{:S(2)}, u32[]{:S(2)}) collective-permute-start(bf16[128,1024]{1,0:T(8,128)(2,1)S(1)} %fusion.2), channel_id=1, source_target_pairs={{0,2},{2,0},{4,6},{6,4},{8,10},{10,8},{12,14},{14,12},{16,18},{18,... | collective-permute-start | bytes 786440 | tf_op jit(solution)/shard_map/ppermute | solution.py:210
  177.5 7.1 %collective-permute-start.14 = (bf16[128,1024]{1,0:T(8,128)(2,1)S(1)}, bf16[128,1024]{1,0:T(8,128)(2,1)S(1)}, u32[]{:S(2)}, u32[]{:S(2)}) collective-permute-start(bf16[128,1024]{1,0:T(8,128)(2,1)S(1)} %fusion.2), channel_id=1, source_target_pairs={{0,4},{2,6},{4,0},{6,2},{8,12},{10,14},{12,8},{14,10},{16,20},{18,... | collective-permute-start | bytes 786440 | tf_op jit(solution)/shard_map/ppermute | solution.py:210
  178.9 11.5 %collective-permute-start.15 = (bf16[128,1024]{1,0:T(8,128)(2,1)S(1)}, bf16[128,1024]{1,0:T(8,128)(2,1)S(1)}, u32[]{:S(2)}, u32[]{:S(2)}) collective-permute-start(bf16[128,1024]{1,0:T(8,128)(2,1)S(1)} %fusion.2), channel_id=1, source_target_pairs={{0,6},{2,4},{4,2},{6,0},{8,14},{10,12},{12,10},{14,8},{16,22},{18,... | collective-permute-start | bytes 786440 | tf_op jit(solution)/shard_map/ppermute | solution.py:210
  180.1 108.4 %collective-permute-start.28 = (bf16[128,1024]{1,0:T(8,128)(2,1)}, bf16[128,1024]{1,0:T(8,128)(2,1)}, u32[]{:S(2)}, u32[]{:S(2)}) collective-permute-start(bf16[128,1024]{1,0:T(8,128)(2,1)} %fusion.4), channel_id=1, source_target_pairs={{0,16},{2,18},{4,20},{6,22},{8,24},{10,26},{12,28},{14,30},{1,17},... | collective-permute-start | bytes 786440 | tf_op jit(solution)/shard_map/ppermute | solution.py:213
  287.2 15.9 %collective-permute-start.19 = (bf16[2,4,256,256]{3,2,1,0:T(8,128)(2,1)}, bf16[2,4,256,256]{3,2,1,0:T(8,128)(2,1)}, u32[]{:S(2)}, u32[]{:S(2)}) collective-permute-start(bf16[2,4,256,256]{3,2,1,0:T(8,128)(2,1)} %broadcast_select_fusion), channel_id=1, source_target_pairs={{0,1},{1,0},{2,3},{3,2},{4,5},{5,4},{6,7},{7,6},{8,9},{9,8},{10,11... | collective-permute-start | bytes 3145736 | tf_op jit(solution)/shard_map/ppermute | solution.py:427
  293.4 3.8 %collective-permute-start.29 = (bf16[256,128]{1,0:T(8,128)(2,1)S(1)}, bf16[256,128]{1,0:T(8,128)(2,1)S(1)}, u32[]{:S(2)}, u32[]{:S(2)}) collective-permute-start(bf16[256,128]{1,0:T(8,128)(2,1)S(1)} %get-tuple-element.48), channel_id=1, source_target_pairs={{0,2},{2,0},{4,6},{6,4},{8,10},{10,8},{12,14},{14,12},{16,18},{18,... | collective-permute-start | bytes 196616 | tf_op jit(solution)/shard_map/ppermute | solution.py:210
  295.0 4.2 %collective-permute-start.31 = (bf16[256,128]{1,0:T(8,128)(2,1)S(1)}, bf16[256,128]{1,0:T(8,128)(2,1)S(1)}, u32[]{:S(2)}, u32[]{:S(2)}) collective-permute-start(bf16[256,128]{1,0:T(8,128)(2,1)S(1)} %get-tuple-element.49), channel_id=1, source_target_pairs={{0,6},{2,4},{4,2},{6,0},{8,14},{10,12},{12,10},{14,8},{16,22},{18,... | collective-permute-start | bytes 196616 | tf_op jit(solution)/shard_map/ppermute | solution.py:210
  299.3 8.3 %collective-permute-start.32 = (f32[2,256,128]{2,1,0:T(8,128)S(1)}, f32[2,256,128]{2,1,0:T(8,128)S(1)}, u32[]{:S(2)}, u32[]{:S(2)}) collective-permute-start(f32[2,256,128]{2,1,0:T(8,128)S(1)} %pad_maximum_fusion.3), channel_id=1, source_target_pairs={{0,1},{1,0},{2,3},{3,2},{4,5},{5,4},{6,7},{7,6},{8,9},{9,8},{10,11... | collective-permute-start | bytes 786440 | tf_op jit(solution)/shard_map/ppermute | solution.py:399
  304.9 8.0 %collective-permute-start.20 = (bf16[2,256,256]{2,1,0:T(8,128)(2,1)S(1)}, bf16[2,256,256]{2,1,0:T(8,128)(2,1)S(1)}, u32[]{:S(2)}, u32[]{:S(2)}) collective-permute-start(bf16[2,256,256]{2,1,0:T(8,128)(2,1)S(1)} %get-tuple-element.43), channel_id=1, source_target_pairs={{0,2},{2,0},{4,6},{6,4},{8,10},{10,8},{12,14},{14,12},{16,18},{18,... | collective-permute-start | bytes 786440 | tf_op jit(solution)/shard_map/ppermute | solution.py:210
  306.3 7.9 %collective-permute-start.21 = (bf16[2,256,256]{2,1,0:T(8,128)(2,1)S(1)}, bf16[2,256,256]{2,1,0:T(8,128)(2,1)S(1)}, u32[]{:S(2)}, u32[]{:S(2)}) collective-permute-start(bf16[2,256,256]{2,1,0:T(8,128)(2,1)S(1)} %get-tuple-element.45), channel_id=1, source_target_pairs={{0,4},{2,6},{4,0},{6,2},{8,12},{10,14},{12,8},{14,10},{16,20},{18,... | collective-permute-start | bytes 786440 | tf_op jit(solution)/shard_map/ppermute | solution.py:210
  306.6 12.8 %collective-permute-start.22 = (bf16[2,256,256]{2,1,0:T(8,128)(2,1)S(1)}, bf16[2,256,256]{2,1,0:T(8,128)(2,1)S(1)}, u32[]{:S(2)}, u32[]{:S(2)}) collective-permute-start(bf16[2,256,256]{2,1,0:T(8,128)(2,1)S(1)} %get-tuple-element.44), channel_id=1, source_target_pairs={{0,6},{2,4},{4,2},{6,0},{8,14},{10,12},{12,10},{14,8},{16,22},{18,... | collective-permute-start | bytes 786440 | tf_op jit(solution)/shard_map/ppermute | solution.py:210
  (71 other events, 1091.6 us)

commit v2 on v0

v2 whole, which is shorter than its diff:
```python
import functools

import jax
import jax.numpy as jnp
from jax import lax
from jax.experimental import pallas as pl
from jax.experimental.pallas import tpu as pltpu
from jax.sharding import PartitionSpec as P

RING = 4
LANES = 128
EXTRA = 16
NT = (((1,), (1,)), ((), ()))
TN = (((0,), (0,)), ((), ()))
NN = (((1,), (0,)), ((), ()))
bf16, f32 = jnp.bfloat16, jnp.float32


def mm(a, b, dims):
    return lax.dot_general(a, b, dims, preferred_element_type=f32)


def mm_exact(a, b, dims):
    return lax.dot_general(a, b, dims, precision=lax.Precision.HIGHEST, preferred_element_type=f32)


def spread(columns, width):
    rows = columns.shape[0]
    return jnp.concatenate(
        [jnp.broadcast_to(columns[:, h : h + 1], (rows, width)) for h in range(columns.shape[1])],
        axis=1,
    )


def iota(shape, axis):
    return lax.broadcasted_iota(jnp.int32, shape, axis)


def three_parts(value):
    first = value.astype(bf16).astype(f32)
    second = (value - first).astype(bf16).astype(f32)
    return first, second, value - first - second


def cumulate(n_heads, log_tiles, cum, cum_t):
    parts = jnp.concatenate([tile[...] for tile in log_tiles], axis=0)
    rows = parts.shape[0]
    source, head = iota((LANES, LANES), 0), iota((LANES, LANES), 1)
    pick = (source < 3 * n_heads) & (lax.rem(source, n_heads) == head)
    logs = mm(parts, pick.astype(f32).astype(bf16), NN)
    upto = (iota((rows, rows), 0) <= iota((rows, rows), 1)).astype(f32)
    cum[...] = mm_exact(upto, logs, TN)
    if cum_t is not None:
        cum_t[...] = mm_exact(logs, upto, TN)


def group_of(value, g, heads, axis):
    shift = lax.rem(LANES - g * heads, LANES)
    value = pltpu.roll(value, shift, axis)
    return value[:, :heads] if axis == 1 else value[:heads]


def diagonal(heads, half, lo, col, row, each):
    later = iota((half, half), 1) >= iota((half, half), 0)
    for h in range(heads):
        log = row[h : h + 1, lo : lo + half] - col[lo : lo + half, h : h + 1]
        each(h, jnp.exp(jnp.where(later, log, -jnp.inf)))


def own_kernel(n_heads, at, x, top, bottom, b, c, log_top, log_bottom, *refs):
    ends, (write_local, read_local, total, cum, cum_t) = refs[:RING], refs[RING:]
    g = pl.program_id(0)
    heads = n_heads // RING
    rows = x.shape[0]
    half = rows // 2
    width = x.shape[1] // heads

    @pl.when(g == 0)
    def _():
        total[...] = jnp.zeros_like(total)
        cumulate(n_heads, (log_top, log_bottom), cum, cum_t)

    col, row = group_of(cum[...], g, heads, 1), group_of(cum_t[...], g, heads, 0)
    mid, last = col[half - 1 : half, :], col[rows - 1 : rows, :]
    for i, dy in enumerate((top, bottom)):
        lo = i * half
        parts = []

        def add(h, decay):
            span = slice(h * width, (h + 1) * width)
            parts.append(decay * mm(x[lo : lo + half, span], dy[:, span], NT))

        diagonal(heads, half, lo, col, row, add)
        total[lo : lo + half, lo : lo + half] += sum(parts)
    xf = x[...].astype(f32)
    early = (xf[:half] * spread(jnp.exp(mid - col[:half]), width)).astype(bf16)
    late = (bottom[...].astype(f32) * spread(jnp.exp(col[half:] - mid), width)).astype(bf16)
    total[:half, half:] += mm(early, late, NT)
    tailed = (xf * spread(jnp.exp(last - col), width)).astype(bf16)
    mine = mm(b[...], tailed, TN).astype(bf16)
    for j in range(RING):

        @pl.when(lax.bitwise_xor(at[0], g) == j)
        def _():
            ends[j][...] = mine

    @pl.when(g == pl.num_programs(0) - 1)
    def _():
        write_local[...] = mm_exact(total[...], c[...].astype(f32), NN)
        read_local[...] = mm_exact(total[...], b[...].astype(f32), TN)


def block_kernel(n_heads, top, bottom, *refs):
    tiles, (act, fronts, log_row, cum_out, cum_t) = refs[:6], refs[6:]
    b = jnp.concatenate([tiles[0][...], tiles[1][...]], axis=0)
    c = jnp.concatenate([tiles[2][...], tiles[3][...]], axis=0)
    g = pl.program_id(0)
    heads = n_heads // RING
    half = top.shape[0]
    rows = 2 * half
    width = top.shape[1] // heads

    @pl.when(g == 0)
    def _():
        cumulate(n_heads, tiles[4:], cum_out, cum_t)

    col, row = group_of(cum_out[...], g, heads, 1), group_of(cum_t[...], g, heads, 0)
    mid, last = col[half - 1 : half, :], col[rows - 1 : rows, :]
    log_row[...] = spread(last, width)
    scores = mm(b, c, NT)
    late_f = bottom[...].astype(f32) * spread(jnp.exp(col[half:] - mid), width)
    late = late_f.astype(bf16)
    first = (top[...].astype(f32) * spread(jnp.exp(col[:half]), width)).astype(bf16)
    second = (late_f * spread(jnp.exp(mid), width)).astype(bf16)
    fronts[0] = (mm(c[:half], first, TN) + mm(c[half:], second, TN)).astype(bf16)
    cross = mm(scores[:half, half:].astype(bf16), late, NN)
    to_mid = jnp.exp(mid - col[:half])
    for i, dy in enumerate((top, bottom)):
        lo = i * half
        score = scores[lo : lo + half, lo : lo + half]

        def put(h, decay):
            span = slice(h * width, (h + 1) * width)
            out = mm((decay * score).astype(bf16), dy[:, span], NN)
            if i == 0:
                out += cross[:, span] * to_mid[:, h : h + 1]
            act[lo : lo + half, span] = out.astype(act.dtype)

        diagonal(heads, half, lo, col, row, put)


def log_over(p, logs, wanted):
    total = jnp.zeros_like(logs[0])
    for k in range(RING):
        total += jnp.where(wanted(lax.bitwise_xor(p, k)), logs[k], 0.0)
    return total


def combine_kernel(way, at, *refs):
    parts, logs, out = refs[:RING], [r[...] for r in refs[RING : 2 * RING]], refs[2 * RING]
    p = at[0]
    n = out.shape[0] - EXTRA
    total = 0.0
    for j in range(RING):
        own = lax.bitwise_xor(p, j)
        if way == 1:
            weight = jnp.exp(log_over(p, logs, lambda k: k > own))
        else:
            weight = jnp.exp(log_over(p, logs, lambda k: k < own))
        part = parts[j][0] if len(parts[j].shape) == 3 else parts[j][...]
        total += part.astype(f32) * weight
    out[:n] = total.astype(bf16)
    write_log(out, sum(logs))


def write_log(out, log):
    n, width = out.shape
    row = iota((EXTRA, width), 0)
    rows = jnp.zeros((EXTRA, width), f32)
    for i, part in enumerate(three_parts(log)):
        rows = jnp.where(row == i, part, rows)
    out[n - EXTRA :] = rows.astype(bf16)


def log_of(message):
    n = message.shape[0] - EXTRA
    tail = message[n:].astype(f32)
    return tail[0:1] + tail[1:2] + tail[2:3]


def merge_kernel(near, far, out):
    n = near.shape[0] - EXTRA
    log = log_of(near)
    out[:n] = (near[:n].astype(f32) + far[:n].astype(f32) * jnp.exp(log)).astype(bf16)
    write_log(out, log + log_of(far))


def ring_kernel(at, *refs):
    fronts, logs, outs = refs[:RING], [r[...] for r in refs[RING : 2 * RING]], refs[2 * RING :]
    p = at[0]
    for j in range(RING):
        own = lax.bitwise_xor(p, j)
        total = 0.0
        for i in range(RING):
            if i != j:
                there = lax.bitwise_xor(p, i)
                weight = jnp.exp(log_over(p, logs, lambda k: (k > own) & (k < there)))
                total += fronts[i][0].astype(f32) * jnp.where(there > own, weight, 0.0)
        outs[j][0] = total.astype(bf16)


def finish_kernel(n_heads, n_w, at, *refs):
    locals_, refs = refs[:RING], refs[RING:]
    rings, refs = refs[:RING], refs[RING:]
    quarters, refs = refs[:RING], refs[RING:]
    logs, refs = [r[...] for r in refs[:RING]], refs[RING:]
    tops, refs = refs[:RING], refs[RING:]
    bottoms, refs = refs[:RING], refs[RING:]
    cums, refs = refs[:RING], refs[RING:]
    w, refs = refs[:n_w], refs[n_w:]
    x, acts, own, write, tiles, total = refs
    g, p = pl.program_id(0), at[0]
    heads = n_heads // RING
    rows = own.shape[0]
    width = own.shape[1] // heads
    n = quarters[0].shape[0] - EXTRA
    source = lax.bitwise_xor(p, g)
    carried = quarters[0][:n].astype(f32)
    for j in range(1, RING):
        carried = jnp.where(source == j, quarters[j][:n].astype(f32), carried)

    @pl.when(g == 0)
    def _():
        write[...] = jnp.zeros_like(write)
        total[...] = jnp.zeros_like(total)

    for j in range(RING):
        col = group_of(cums[j][...], g, heads, 1)
        tail = spread(jnp.exp(col[rows - 1 : rows, :] - col), width)
        place = lax.bitwise_xor(p, j)
        weight = jnp.exp(log_over(p, logs, lambda k: k > place))
        grads = (carried * weight + rings[j][0].astype(f32)).astype(bf16)
        b = jnp.concatenate([tops[j][...], bottoms[j][...]], axis=0)
        out = mm(b, grads, NN) * tail + locals_[j][...].astype(f32)
        out = out.astype(acts.dtype)
        acts[j * rows : (j + 1) * rows, :] = out
        if j == 0:
            own[...] = out
            write[...] += mm((x[...].astype(f32) * tail).astype(bf16), grads, NT)
    for k in range(n_w):
        n_rows = w[k].shape[0]
        total[:, k * n_rows : (k + 1) * n_rows] += mm(acts[...], w[k][...], NT)

    @pl.when(g == pl.num_programs(0) - 1)
    def _():
        tiles[...] = total[...].astype(tiles.dtype)


def read_kernel(n_heads, at, *refs):
    tops, refs = refs[:RING], refs[RING:]
    bottoms, refs = refs[:RING], refs[RING:]
    cums, refs = refs[:RING], refs[RING:]
    logs, refs = [r[...] for r in refs[:RING]], refs[RING:]
    ends, (carried, *outs) = refs[:RING], refs[RING:]
    p = at[0]
    heads = n_heads // RING
    half = tops[0].shape[0]
    n = carried.shape[0] - EXTRA
    width = carried.shape[1] // heads
    for j in range(RING):
        own = lax.bitwise_xor(p, j)
        total = carried[:n].astype(f32) * jnp.exp(log_over(p, logs, lambda k: k < own))
        for i in range(RING):
            if i != j:
                there = lax.bitwise_xor(p, i)
                weight = jnp.exp(log_over(p, logs, lambda k: (k < own) & (k > there)))
                total += ends[i][...].astype(f32) * jnp.where(there < own, weight, 0.0)
        states = total.astype(bf16)
        decay = spread(jnp.exp(group_of(cums[j][...], p, heads, 1)), width)
        for i, dy in enumerate((tops[j], bottoms[j])):
            at_rows = slice(i * half, (i + 1) * half)
            scaled = (dy[...].astype(f32) * decay[at_rows]).astype(bf16)
            outs[j][at_rows] = mm(scaled, states, NT).astype(bf16)


def place_kernel(outer, share, at, *refs):
    blocks, out = refs[:-1], refs[-1]
    p, z, side = at[0], at[1], at[2]
    width = out.shape[1] // (share * RING)
    for k in range(outer):
        o = lax.rem(z + k, outer)
        first = lax.rem(o, share) * RING

        @pl.when(lax.div(o, share) == side)
        def _():
            for j in range(RING):
                column = pl.multiple_of((first + lax.bitwise_xor(p, j)) * width, width)
                if k < outer - 1:
                    out[:, pl.ds(column, width)] = blocks[j][:, k * width : (k + 1) * width]
                else:
                    out[:, pl.ds(column, width)] = blocks[RING + j][...]


def call(kernel, name, grid, in_specs, out_specs, out_shape, scratch=(), prefetch=1):
    return pl.pallas_call(
        kernel,
        grid_spec=pltpu.PrefetchScalarGridSpec(
            num_scalar_prefetch=prefetch,
            grid=grid,
            in_specs=in_specs,
            out_specs=out_specs,
            scratch_shapes=list(scratch),
        ),
        out_shape=out_shape,
        compiler_params=pltpu.CompilerParams(vmem_limit_bytes=56 * 2**20),
        cost_estimate=pl.CostEstimate(flops=0, bytes_accessed=0, transcendentals=0),
        name=name,
    )


def local(x, dy, write_proj, read_proj, log_decay, w_in):
    rows, columns = x.shape
    half = rows // 2
    state_dim = write_proj.shape[1]
    n_heads = log_decay.shape[1]
    heads = n_heads // RING
    width = columns // n_heads
    part = heads * width
    w_rows = w_in.shape[0]
    n_seq, n_head = lax.axis_size("seq"), lax.axis_size("head")
    outer = n_seq // RING
    place = lax.axis_index("seq")
    side = lax.axis_index("head")
    p, z = place % RING, place // RING
    at = p.astype(jnp.int32)[None]

    def swap(value, j):
        return lax.ppermute(value, "seq", [(s, s ^ j) for s in range(n_seq)])

    def along(value, d):
        return lax.ppermute(
            value, "seq", [(s, s + d * RING) for s in range(n_seq) if 0 <= s + d * RING < n_seq]
        )

    w_blocks = [w_in]

    def turn_w():
        turn = [(s, (s - RING) % n_seq) for s in range(n_seq)]
        w_blocks.append(lax.ppermute(w_blocks[-1], "seq", turn))

    turn_w()

    first = lax.reduce_precision(log_decay, 8, 7)
    second = lax.reduce_precision(log_decay - first, 8, 7)
    third = log_decay - first - second
    fill = jnp.zeros((rows, LANES - 3 * n_heads), bf16)
    beside = [write_proj, read_proj] + [v.astype(bf16) for v in (first, second, third)] + [fill]
    own_top = jnp.concatenate([v[:half] for v in [dy] + beside], axis=1)
    own_bottom = jnp.concatenate([v[half:] for v in [dy] + beside], axis=1)
    x_top, y_bottom = swap(own_top, 1), swap(own_bottom, 2)
    x_bottom, y_top = swap(own_bottom, 1), swap(own_top, 2)
    x_top, x_bottom, y_top, y_bottom = lax.optimization_barrier((x_top, x_bottom, y_top, y_bottom))
    blocks = [
        (own_top, own_bottom),
        (x_top, x_bottom),
        (y_top, y_bottom),
        (swap(x_top, 2), swap(y_bottom, 1)),
    ]

    half_spec = pl.BlockSpec((half, part), lambda g, q: (0, g))
    first_tile = columns // LANES

    def tile_spec(i):
        return pl.BlockSpec((half, LANES), lambda g, q: (0, first_tile + i))

    def const(*shape):
        return pl.BlockSpec(shape, lambda g, q: (0,) * len(shape))

    by_group = pl.BlockSpec((rows, part), lambda g, q: (0, g))
    state_spec = pl.BlockSpec((1, state_dim, part), lambda g, q: (g, 0, 0))
    log_spec = pl.BlockSpec((1, part), lambda g, q: (0, g))
    cum_spec = const(rows, LANES)
    proj_spec = const(rows, state_dim)
    message_spec = const(state_dim + EXTRA, part)
    shape = jax.ShapeDtypeStruct
    state_shape = shape((RING, state_dim, part), bf16)
    log_shape = shape((1, columns), f32)
    cum_shape = shape((rows, LANES), f32)
    message_shape = shape((state_dim + EXTRA, part), bf16)
    cum_scratch, cum_t_scratch = pltpu.VMEM((rows, LANES), f32), pltpu.VMEM((LANES, rows), f32)

    *ends, write_local, read_local = call(
        functools.partial(own_kernel, n_heads),
        "own_tokens",
        (RING,),
        [by_group, half_spec, half_spec, proj_spec, proj_spec, tile_spec(2), tile_spec(2)],
        [const(state_dim, part)] * RING + [proj_spec] * 2,
        [shape((state_dim, part), bf16)] * RING + [shape((rows, state_dim), f32)] * 2,
        [pltpu.VMEM((rows, rows), f32), cum_scratch, cum_t_scratch],
    )(at, x, own_top, own_bottom, write_proj, read_proj, own_top, own_bottom)

    def block(j):
        top, bottom = blocks[j]
        return call(
            functools.partial(lambda *refs: block_kernel(n_heads, *refs[1:])),
            "tokens",
            (RING,),
            [half_spec, half_spec] + [tile_spec(i) for i in range(3) for _ in range(2)],
            [by_group, state_spec, log_spec, cum_spec],
            [shape((rows, columns), bf16), state_shape, log_shape, cum_shape],
            [cum_t_scratch],
        )(at, top, bottom, *([top, bottom] * 3))

    results = [block(0)]
    logs = [results[0][2]]
    logs[0], read_local, w_blocks[-1] = lax.optimization_barrier(
        (logs[0], read_local, w_blocks[-1])
    )
    results += [block(j) for j in range(1, RING - 1)]
    logs += [v[2] for v in results[1:]]
    logs, blocks[-1] = lax.optimization_barrier((logs, blocks[-1]))
    results.append(block(RING - 1))
    logs.append(results[-1][2])
    local_acts, fronts, _, cums = zip(*results)

    mine3 = pl.BlockSpec((1, state_dim, part), lambda g, q: (q[0], 0, 0))
    mine_log = pl.BlockSpec((1, part), lambda g, q: (0, q[0]))

    def combine(parts, way):
        return call(
            functools.partial(combine_kernel, way),
            "message",
            (1,),
            [mine3 if v.ndim == 3 else const(*v.shape) for v in parts] + [mine_log] * RING,
            message_spec,
            message_shape,
        )(at, *parts, *logs)

    def merge(near, far):
        return call(
            lambda q, *refs: merge_kernel(*refs),
            "merge",
            (1,),
            [message_spec] * 2,
            message_spec,
            message_shape,
        )(at, near, far)

    fronts = list(fronts)
    while len(w_blocks) < min(3, outer):
        turn_w()
    fronts[-1], w_blocks[-1] = lax.optimization_barrier((fronts[-1], w_blocks[-1]))
    while len(w_blocks) < outer:
        turn_w()

    def scan_along(span, way, after=None):
        result, d = None, 1
        while d < outer:
            got = along(span, way * d)
            if after is not None:
                got = after(got)
            result = got if result is None else merge(result, got)
            if 2 * d < outer:
                span = merge(span, got)
            d *= 2
        return result

    grad_part = scan_along(combine(fronts, -1), -1)
    grad_parts = [grad_part] + [swap(grad_part, j) for j in range(1, RING)]

    ring_grads = call(
        ring_kernel,
        "ring_grads",
        (RING,),
        [state_spec] * RING + [log_spec] * RING,
        [state_spec] * RING,
        [state_shape] * RING,
    )(at, *fronts, *logs)

    n_w = outer - 1
    tall = pl.BlockSpec((RING * rows, part), lambda g, q: (0, g))
    w_spec = pl.BlockSpec((w_rows, part), lambda g, q: (0, g))
    acts, act_grad, write_carry, tiles = call(
        functools.partial(finish_kernel, n_heads, n_w),
        "finish",
        (RING,),
        [by_group] * RING
        + [state_spec] * RING
        + [message_spec] * RING
        + [log_spec] * RING
        + [tile_spec(0)] * (2 * RING)
        + [cum_spec] * RING
        + [w_spec] * n_w
        + [by_group],
        [tall, by_group, proj_spec, const(RING * rows, n_w * w_rows)],
        [
            shape((RING * rows, columns), bf16),
            shape((rows, columns), bf16),
            shape((rows, state_dim), f32),
            shape((RING * rows, n_w * w_rows), bf16),
        ],
        [pltpu.VMEM((RING * rows, n_w * w_rows), f32)],
    )(
        at,
        *local_acts,
        *ring_grads,
        *grad_parts,
        *logs,
        *[top for top, _ in blocks],
        *[bottom for _, bottom in blocks],
        *cums,
        *w_blocks[:n_w],
        x,
    )

    def over_head(tile):
        if n_head == 2:
            got = lax.ppermute(tile, "head", [(0, 1), (1, 0)])
            return (tile.astype(f32) + got.astype(f32)).astype(bf16)
        return lax.psum(tile.astype(f32), "head").astype(bf16)

    def to_owners(tile):
        return [tile[:rows]] + [swap(tile[j * rows : (j + 1) * rows], j) for j in range(1, RING)]

    share = outer // n_head
    tiles, w_blocks[-1] = lax.optimization_barrier((tiles, w_blocks[-1]))
    early = over_head(tiles)
    late_tile = mm(acts, w_blocks[-1], NT).astype(bf16)

    held = [tiles, late_tile]

    def after(got):
        held[0], got = lax.optimization_barrier((held[0], got))
        held[0] = held[1]
        return got

    my_ends = [ends[0]] + [swap(ends[j], j) for j in range(1, RING)]
    state_part = scan_along(combine(my_ends, 1), 1, after)
    mine_half = pl.BlockSpec((half, part), lambda g, q: (0, q[0]))
    read_parts = call(
        functools.partial(read_kernel, n_heads),
        "read_carry",
        (1,),
        [mine_half] * (2 * RING)
        + [cum_spec] * RING
        + [mine_log] * RING
        + [const(state_dim, part)] * RING
        + [message_spec],
        [proj_spec] * RING,
        [shape((rows, state_dim), bf16)] * RING,
    )(
        at,
        *[top for top, _ in blocks],
        *[bottom for _, bottom in blocks],
        *cums,
        *logs,
        *my_ends,
        state_part,
    )

    late = over_head(late_tile)
    late, read_parts = lax.optimization_barrier((late, read_parts))
    late = to_owners(late)
    early = to_owners(early)
    read_carry = read_parts[0].astype(f32) + sum(
        swap(read_parts[j], j).astype(f32) for j in range(1, RING)
    )
    both = jnp.stack([write_local + write_carry, read_local + read_carry])
    if n_head == 2:
        both = both + lax.ppermute(both, "head", [(0, 1), (1, 0)])
    else:
        both = lax.psum(both, "head")

    if w_rows % LANES == 0:
        input_grad = pl.pallas_call(
            functools.partial(place_kernel, outer, share),
            in_specs=[pl.BlockSpec(memory_space=pltpu.SMEM)]
            + [pl.BlockSpec(memory_space=pltpu.VMEM)] * (2 * RING),
            out_specs=pl.BlockSpec(memory_space=pltpu.VMEM),
            out_shape=shape((rows, share * RING * w_rows), bf16),
            compiler_params=pltpu.CompilerParams(vmem_limit_bytes=32 * 2**20),
            name="place",
        )(jnp.stack([p, z, side]).astype(jnp.int32), *early, *late)
    else:
        order = p ^ jnp.arange(RING)
        pieces = jnp.concatenate([jnp.stack(early), jnp.stack(late)], axis=2)
        pieces = jnp.take(pieces.reshape(RING, rows, outer, w_rows), order, axis=0)
        pieces = jnp.take(pieces, (side * share + jnp.arange(share) - z) % outer, axis=2)
        input_grad = pieces.transpose(1, 2, 0, 3).reshape(rows, share * RING * w_rows)
    return (input_grad, act_grad, both[0], both[1])


def solution(mesh):
    return jax.shard_map(
        local,
        mesh=mesh,
        in_specs=(
            P("seq", "head"),
            P("seq", "head"),
            P("seq", None),
            P("seq", None),
            P("seq", "head"),
            P("seq", "head"),
        ),
        out_specs=(P("seq", "head"), P("seq", "head"), P("seq", None), P("seq", None)),
        check_vma=False,
    )
```

time: 972 us -> 291 us (0.30)
  the two profiles are of different devices: /device:TPU:1 before, /device:TPU:24 now
where the time goes in v2:
time: 291 us; the launch traced here: 290 us
  waiting for transfers between devices  144 us (49%)
  Pallas kernels  83 us (29%)
  starting transfers between devices  36.8 us (13%)
  local copies, waits for them, and re-layouts  16.7 us (6%)
  matrix products  6.39 us (2%)
    ppermute x4, waiting for transfers between devices, along(): lax.ppermute(value, 'seq', [(s, s + d * RING) for s in range(n_seq) if 0...  69.6 us
    ppermute x21, waiting for transfers between devices, swap(): return lax.ppermute(value, 'seq', [(s, s ^ j) for s in range(n_seq)])  56.1 us
    pallas_call x4, Pallas kernels, block(): call(functools.partial(lambda *refs: block_kernel(n_heads, *refs[1:])), '...  29.1 us
    ppermute x21, starting transfers between devices, swap(): return lax.ppermute(value, 'seq', [(s, s ^ j) for s in range(n_seq)])  24.8 us
    pallas_call x1, Pallas kernels, local(): call(functools.partial(finish_kernel, n_heads, n_w), 'finish', (RING,), [...  20.2 us
    ppermute x3, waiting for transfers between devices, turn_w(): w_blocks.append(lax.ppermute(w_blocks[-1], 'seq', turn))  18.3 us
    ppermute x4, starting transfers between devices, along(): lax.ppermute(value, 'seq', [(s, s + d * RING) for s in range(n_seq) if 0...  10.4 us
    pallas_call x1, Pallas kernels, local(): call(functools.partial(own_kernel, n_heads), 'own_tokens', (RING,), [by_g...  9.32 us
  transfers between devices with their start and end apart: 31, of which 13 were waited for; matrix products, arithmetic and copies ran while one was open for 6% of the time, Pallas kernels for 28%

profile of v2, /device:TPU:24, one launch (start us, length us, event | category | flops | bytes accessed | tf_op | source)
XLA Modules:
  0.0 289.5 jit_solution(3402696497826119600)
XLA Ops:
  5.0 2.7 fusion.2
  8.8 1.6 collective-permute-start
  10.3 2.3 concatenate.7.refs_2_.refs_4_.refs_6_.refs_8_.bottom.log_bottom.refs_20_
  13.2 1.5 collective-permute-start.2
  15.3 7.3 %tokens.4 = (bf16[256,4096]{1,0:T(8,128)(2,1)}, bf16[4,128,1024]{2,1,0:T(8,128)(2,1)}, f32[1,4096]{1,0:T(1,128)}, f32[256,128]{1,0:T(8,128)}) custom-call(s32[1]{0:T(128)} %bitcast.refs_0_.at.q, bf16[128,4480]{1,0:T(8,128)(2,1)} %copy-done, bf16[128,4480]{1,0:T(8,128)(2,1)} %copy-done.1, bf16[128,4480]{1,0:T(8,128)(2,1)} %copy-done, ...), custom_call_target="tpu_custom_call" | custom-call | tf_op jit(solution)/shard_map/tokens/pallas_call | solution.py:404
  22.6 9.3 %own_tokens.1 = (bf16[128,1024]{1,0:T(8,128)(2,1)}, bf16[128,1024]{1,0:T(8,128)(2,1)}, bf16[128,1024]{1,0:T(8,128)(2,1)}, bf16[128,1024]{1,0:T(8,128)(2,1)}, f32[256,128]{1,0:T(8,128)}, /*index=5*/f32[256,128]{1,0:T(8,128)}) custom-call(s32[1]{0:T(128)} %bitcast.refs_0_.at.q, bf16[256,4096]{1,0:T(8,128)(2,1)} %refs_31_.1, bf16[128,4480]{1,0:T(8,128)(2,1)} %copy-done, ...), custom_call_target="tpu_custom_call" | custom-call | tf_op jit(solution)/shard_map/own_tokens/pallas_call | solution.py:392
  31.9 18.3 %collective-permute-done.4.refs_29_ = bf16[256,4096]{1,0:T(8,128)(2,1)} collective-permute-done((bf16[256,4096]{1,0:T(8,128)(2,1)}, bf16[256,4096]{1,0:T(8,128)(2,1)}, u32[]{:S(2)}, u32[]{:S(2)}) %collective-permute-start.4) | collective-permute-done | bytes 2097184 | tf_op jit(solution)/shard_map/ppermute | solution.py:349
  50.2 10.1 %collective-permute-done.1.refs_2_.refs_4_.refs_6_.refs_8_.refs_21_.refs_5_ = bf16[128,4480]{1,0:T(8,128)(2,1)} collective-permute-done((bf16[128,4480]{1,0:T(8,128)(2,1)S(1)}, bf16[128,4480]{1,0:T(8,128)(2,1)}, u32[]{:S(2)}, u32[]{:S(2)}) %collective-permute-start.1) | collective-permute-done | bytes 1146912 | tf_op jit(solution)/shard_map/ppermute | solution.py:338
  60.3 3.9 %collective-permute-done.3.refs_2_.refs_4_.refs_6_.refs_8_.refs_22_ = bf16[128,4480]{1,0:T(8,128)(2,1)} collective-permute-done((bf16[128,4480]{1,0:T(8,128)(2,1)S(1)}, bf16[128,4480]{1,0:T(8,128)(2,1)}, u32[]{:S(2)}, u32[]{:S(2)}) %collective-permute-start.3) | collective-permute-done | bytes 1146912 | tf_op jit(solution)/shard_map/ppermute | solution.py:338
  67.1 7.3 %tokens.5 = (bf16[256,4096]{1,0:T(8,128)(2,1)}, bf16[4,128,1024]{2,1,0:T(8,128)(2,1)}, f32[1,4096]{1,0:T(1,128)}, f32[256,128]{1,0:T(8,128)}) custom-call(s32[1]{0:T(128)} %bitcast.refs_0_.at.q, bf16[128,4480]{1,0:T(8,128)(2,1)} %copy-done.2, bf16[128,4480]{1,0:T(8,128)(2,1)} %collective-permute-done.1.refs_2_.refs_4_.refs_6_.refs_8_.refs_21_.refs_5_, ...), custom_call_target="tpu_custom_call" | custom-call | tf_op jit(solution)/shard_map/tokens/pallas_call | solution.py:404
  74.4 7.3 %tokens.6 = (bf16[256,4096]{1,0:T(8,128)(2,1)}, bf16[4,128,1024]{2,1,0:T(8,128)(2,1)}, f32[1,4096]{1,0:T(1,128)}, f32[256,128]{1,0:T(8,128)}) custom-call(s32[1]{0:T(128)} %bitcast.refs_0_.at.q, bf16[128,4480]{1,0:T(8,128)(2,1)} %collective-permute-done.2.refs_1_.refs_3_.refs_5_.refs_7_.refs_18_.refs_2_, ...), custom_call_target="tpu_custom_call" | custom-call | tf_op jit(solution)/shard_map/tokens/pallas_call | solution.py:404
  81.7 7.8 %collective-permute-done.5.refs_1_.refs_3_.refs_5_.refs_7_.refs_19_ = bf16[128,4480]{1,0:T(8,128)(2,1)S(1)} collective-permute-done((bf16[128,4480]{1,0:T(8,128)(2,1)S(1)}, bf16[128,4480]{1,0:T(8,128)(2,1)S(1)}, u32[]{:S(2)}, u32[]{:S(2)}) %collective-permute-start.5) | collective-permute-done | bytes 1146912 | tf_op jit(solution)/shard_map/ppermute | solution.py:338
  91.9 7.2 %tokens.7 = (bf16[256,4096]{1,0:T(8,128)(2,1)}, bf16[4,128,1024]{2,1,0:T(8,128)(2,1)}, f32[1,4096]{1,0:T(1,128)}, f32[256,128]{1,0:T(8,128)}) custom-call(s32[1]{0:T(128)} %bitcast.refs_0_.at.q, bf16[128,4480]{1,0:T(8,128)(2,1)} %copy-done.3, bf16[128,4480]{1,0:T(8,128)(2,1)} %copy-done.4, bf16[128,4480]{1,0:T(8,128)(2,1)} %copy-done.3, ...), custom_call_target="tpu_custom_call" | custom-call | tf_op jit(solution)/shard_map/tokens/pallas_call | solution.py:404
  99.7 2.4 message.2.refs_0_
  102.1 2.4 collective-permute-start.8
  104.5 44.0 %collective-permute-done.8.refs_1_.refs_0_ = bf16[144,1024]{1,0:T(8,128)(2,1)S(1)} collective-permute-done((bf16[144,1024]{1,0:T(8,128)(2,1)}, bf16[144,1024]{1,0:T(8,128)(2,1)S(1)}, u32[]{:S(2)}, u32[]{:S(2)}) %collective-permute-start.8) | collective-permute-done | bytes 294944 | tf_op jit(solution)/shard_map/ppermute | solution.py:341
  149.2 1.9 merge.4
  151.1 5.2 %collective-permute-start.9 = (bf16[144,1024]{1,0:T(8,128)(2,1)}, bf16[144,1024]{1,0:T(8,128)(2,1)S(1)}, u32[]{:S(2)}, u32[]{:S(2)}) collective-permute-start(bf16[144,1024]{1,0:T(8,128)(2,1)} %merge.4), channel_id=1, source_target_pairs={{16,0},{18,2},{20,4},{22,6},{24,8},{26,10},{28,12},{30,14},{17,1},... | collective-permute-start | bytes 884744 | tf_op jit(solution)/shard_map/ppermute | solution.py:341
  158.4 2.3 collective-permute-done.9.refs_1_
  161.4 1.9 merge.5.refs_8_
  168.3 13.0 %collective-permute-done.21.refs_3_.refs_19_ = bf16[128,1024]{1,0:T(8,128)(2,1)S(1)} collective-permute-done((bf16[128,1024]{1,0:T(8,128)(2,1)S(1)}, bf16[128,1024]{1,0:T(8,128)(2,1)S(1)}, u32[]{:S(2)}, u32[]{:S(2)}) %collective-permute-start.21) | collective-permute-done | bytes 262176 | tf_op jit(solution)/shard_map/ppermute | solution.py:338
  181.9 2.1 message.3.refs_0_
  185.4 5.5 %ring_grads.1 = (bf16[4,128,1024]{2,1,0:T(8,128)(2,1)}, bf16[4,128,1024]{2,1,0:T(8,128)(2,1)}, bf16[4,128,1024]{2,1,0:T(8,128)(2,1)}, bf16[4,128,1024]{2,1,0:T(8,128)(2,1)}) custom-call(s32[1]{0:T(128)} %bitcast.refs_0_.at.q, bf16[4,128,1024]{2,1,0:T(8,128)(2,1)} %get-tuple-element.76.refs_0_, bf16[4,128,1024]{2,1,0:T(8,128)(2,1)} %get-tuple-element.77.refs_1_, ...), custom_call_target="tpu_custom_call" | custom-call | tf_op jit(solution)/shard_map/ring_grads/pallas_call | solution.py:471
  191.8 20.2 %finish.1 = (bf16[1024,4096]{1,0:T(8,128)(2,1)}, bf16[256,4096]{1,0:T(8,128)(2,1)}, f32[256,128]{1,0:T(8,128)}, bf16[1024,768]{1,0:T(8,128)(2,1)}) custom-call(s32[1]{0:T(128)} %bitcast.refs_0_.at.q, bf16[256,4096]{1,0:T(8,128)(2,1)} %get-tuple-element.61.refs_0_, bf16[256,4096]{1,0:T(8,128)(2,1)} %get-tuple-element.64.refs_1_, ...), custom_call_target="tpu_custom_call" | custom-call | tf_op jit(solution)/shard_map/finish/pallas_call | solution.py:483
  213.3 6.4 %convolution_convert_fusion = bf16[1024,256]{1,0:T(8,128)(2,1)S(1)} fusion(bf16[1024,4096]{1,0:T(8,128)(2,1)} %get-tuple-element.97, bf16[256,4096]{1,0:T(8,128)(2,1)} %copy-done.21), kind=kOutput, calls=%fused_computation.1 | convolution fusion | flops 2147745792 | bytes 11010048 | tf_op jit(solution)/shard_map/dot_general | solution.py:20
  221.0 1.9 merge.6
  224.5 23.3 %collective-permute-done.23.refs_1_ = bf16[144,1024]{1,0:T(8,128)(2,1)S(1)} collective-permute-done((bf16[144,1024]{1,0:T(8,128)(2,1)}, bf16[144,1024]{1,0:T(8,128)(2,1)S(1)}, u32[]{:S(2)}, u32[]{:S(2)}) %collective-permute-start.23) | collective-permute-done | bytes 294944 | tf_op jit(solution)/shard_map/ppermute | solution.py:341
  248.5 1.9 merge.7.refs_20_
  250.4 5.2 %read_carry.1 = (bf16[256,128]{1,0:T(8,128)(2,1)}, bf16[256,128]{1,0:T(8,128)(2,1)}, bf16[256,128]{1,0:T(8,128)(2,1)}, bf16[256,128]{1,0:T(8,128)(2,1)}) custom-call(s32[1]{0:T(128)} %bitcast.refs_0_.at.q, bf16[128,4480]{1,0:T(8,128)(2,1)} %copy-done, bf16[128,4480]{1,0:T(8,128)(2,1)} %copy-done.2, ...), custom_call_target="tpu_custom_call" | custom-call | tf_op jit(solution)/shard_map/read_carry/pallas_call | solution.py:540
  255.8 1.6 collective-permute-start.29
  270.1 17.6 %collective-permute-done.26.refs_7_ = bf16[256,256]{1,0:T(8,128)(2,1)S(1)} collective-permute-done((bf16[256,256]{1,0:T(8,128)(2,1)S(1)}, bf16[256,256]{1,0:T(8,128)(2,1)S(1)}, u32[]{:S(2)}, u32[]{:S(2)}) %collective-permute-start.26) | collective-permute-done | bytes 131104 | tf_op jit(solution)/shard_map/ppermute | solution.py:338
  287.8 1.7 place.1
  (117 shorter events, 41.7 us)
Async XLA Ops:
  0.6 49.5 %collective-permute-start.4 = (bf16[256,4096]{1,0:T(8,128)(2,1)}, bf16[256,4096]{1,0:T(8,128)(2,1)}, u32[]{:S(2)}, u32[]{:S(2)}) collective-permute-start(bf16[256,4096]{1,0:T(8,128)(2,1)} %refs_28_.1), channel_id=1, source_target_pairs={{0,24},{2,26},{4,28},{6,30},{8,0},{10,2},{12,4},{14,6},{16,8},{18,... | collective-permute-start | bytes 6291464 | tf_op jit(solution)/shard_map/ppermute | solution.py:349
  8.8 41.4 %collective-permute-start = (bf16[128,4480]{1,0:T(8,128)(2,1)S(1)}, bf16[128,4480]{1,0:T(8,128)(2,1)S(1)}, u32[]{:S(2)}, u32[]{:S(2)}) collective-permute-start(bf16[128,4480]{1,0:T(8,128)(2,1)S(1)} %concatenate.6.refs_1_.refs_3_.refs_5_.refs_7_.top.log_top.refs_16_.refs_0_), channel_id=1, source_target_pairs={{0,2},{2,0},{4,6},{6,4},{8,10},{10,8},{12,14},{14,12},{16,18},{18,... | collective-permute-start | bytes 3440648 | tf_op jit(solution)/shard_map/ppermute | solution.py:338
  12.6 47.6 %collective-permute-start.1 = (bf16[128,4480]{1,0:T(8,128)(2,1)S(1)}, bf16[128,4480]{1,0:T(8,128)(2,1)}, u32[]{:S(2)}, u32[]{:S(2)}) collective-permute-start(bf16[128,4480]{1,0:T(8,128)(2,1)S(1)} %concatenate.7.refs_2_.refs_4_.refs_6_.refs_8_.bottom.log_bottom.refs_20_), channel_id=1, source_target_pairs={{0,2},{2,0},{4,6},{6,4},{8,10},{10,8},{12,14},{14,12},{16,18},{18,... | collective-permute-start | bytes 3440648 | tf_op jit(solution)/shard_map/ppermute | solution.py:338
  13.2 47.0 %collective-permute-start.2 = (bf16[128,4480]{1,0:T(8,128)(2,1)S(1)}, bf16[128,4480]{1,0:T(8,128)(2,1)}, u32[]{:S(2)}, u32[]{:S(2)}) collective-permute-start(bf16[128,4480]{1,0:T(8,128)(2,1)S(1)} %concatenate.6.refs_1_.refs_3_.refs_5_.refs_7_.top.log_top.refs_16_.refs_0_), channel_id=1, source_target_pairs={{0,4},{2,6},{4,0},{6,2},{8,12},{10,14},{12,8},{14,10},{16,20},{18,... | collective-permute-start | bytes 3440648 | tf_op jit(solution)/shard_map/ppermute | solution.py:338
  14.8 49.4 %collective-permute-start.3 = (bf16[128,4480]{1,0:T(8,128)(2,1)S(1)}, bf16[128,4480]{1,0:T(8,128)(2,1)}, u32[]{:S(2)}, u32[]{:S(2)}) collective-permute-start(bf16[128,4480]{1,0:T(8,128)(2,1)S(1)} %concatenate.7.refs_2_.refs_4_.refs_6_.refs_8_.bottom.log_bottom.refs_20_), channel_id=1, source_target_pairs={{0,4},{2,6},{4,0},{6,2},{8,12},{10,14},{12,8},{14,10},{16,20},{18,... | collective-permute-start | bytes 3440648 | tf_op jit(solution)/shard_map/ppermute | solution.py:338
  50.2 49.0 %collective-permute-start.7 = (bf16[256,4096]{1,0:T(8,128)(2,1)}, bf16[256,4096]{1,0:T(8,128)(2,1)S(1)}, u32[]{:S(2)}, u32[]{:S(2)}) collective-permute-start(bf16[256,4096]{1,0:T(8,128)(2,1)} %collective-permute-done.4.refs_29_), channel_id=1, source_target_pairs={{0,24},{2,26},{4,28},{6,30},{8,0},{10,2},{12,4},{14,6},{16,8},{18,... | collective-permute-start | bytes 6291464 | tf_op jit(solution)/shard_map/ppermute | solution.py:349
  64.2 25.3 %collective-permute-start.5 = (bf16[128,4480]{1,0:T(8,128)(2,1)S(1)}, bf16[128,4480]{1,0:T(8,128)(2,1)S(1)}, u32[]{:S(2)}, u32[]{:S(2)}) collective-permute-start(bf16[128,4480]{1,0:T(8,128)(2,1)S(1)} %collective-permute-done.refs_1_.refs_3_.refs_5_.refs_7_.refs_17_), channel_id=1, source_target_pairs={{0,4},{2,6},{4,0},{6,2},{8,12},{10,14},{12,8},{14,10},{16,20},{18,... | collective-permute-start | bytes 3440648 | tf_op jit(solution)/shard_map/ppermute | solution.py:338
  65.7 25.2 %collective-permute-start.6 = (bf16[128,4480]{1,0:T(8,128)(2,1)}, bf16[128,4480]{1,0:T(8,128)(2,1)S(1)}, u32[]{:S(2)}, u32[]{:S(2)}) collective-permute-start(bf16[128,4480]{1,0:T(8,128)(2,1)} %collective-permute-done.3.refs_2_.refs_4_.refs_6_.refs_8_.refs_22_), channel_id=1, source_target_pairs={{0,2},{2,0},{4,6},{6,4},{8,10},{10,8},{12,14},{14,12},{16,18},{18,... | collective-permute-start | bytes 3440648 | tf_op jit(solution)/shard_map/ppermute | solution.py:338
  99.2 112.8 %collective-permute-start.13 = (bf16[256,4096]{1,0:T(8,128)(2,1)S(1)}, bf16[256,4096]{1,0:T(8,128)(2,1)S(1)}, u32[]{:S(2)}, u32[]{:S(2)}) collective-permute-start(bf16[256,4096]{1,0:T(8,128)(2,1)S(1)} %collective-permute-done.7.refs_30_), channel_id=1, source_target_pairs={{0,24},{2,26},{4,28},{6,30},{8,0},{10,2},{12,4},{14,6},{16,8},{18,... | collective-permute-start | bytes 6291464 | tf_op jit(solution)/shard_map/ppermute | solution.py:349
  99.7 67.1 %copy-start.22 = (bf16[128,1024]{1,0:T(8,128)(2,1)S(1)}, bf16[128,1024]{1,0:T(8,128)(2,1)}, u32[]{:S(2)}) copy-start(bf16[128,1024]{1,0:T(8,128)(2,1)} %get-tuple-element.102) | copy-start | bytes 786436
  102.1 46.4 %collective-permute-start.8 = (bf16[144,1024]{1,0:T(8,128)(2,1)}, bf16[144,1024]{1,0:T(8,128)(2,1)S(1)}, u32[]{:S(2)}, u32[]{:S(2)}) collective-permute-start(bf16[144,1024]{1,0:T(8,128)(2,1)} %message.2.refs_0_), channel_id=1, source_target_pairs={{8,0},{10,2},{12,4},{14,6},{16,8},{18,10},{20,12},{22,14},{24,16},... | collective-permute-start | bytes 884744 | tf_op jit(solution)/shard_map/ppermute | solution.py:341
  151.1 9.6 %collective-permute-start.9 = (bf16[144,1024]{1,0:T(8,128)(2,1)}, bf16[144,1024]{1,0:T(8,128)(2,1)S(1)}, u32[]{:S(2)}, u32[]{:S(2)}) collective-permute-start(bf16[144,1024]{1,0:T(8,128)(2,1)} %merge.4), channel_id=1, source_target_pairs={{16,0},{18,2},{20,4},{22,6},{24,8},{26,10},{28,12},{30,14},{17,1},... | collective-permute-start | bytes 884744 | tf_op jit(solution)/shard_map/ppermute | solution.py:341
  156.3 9.0 %collective-permute-start.19 = (bf16[128,1024]{1,0:T(8,128)(2,1)S(1)}, bf16[128,1024]{1,0:T(8,128)(2,1)S(1)}, u32[]{:S(2)}, u32[]{:S(2)}) collective-permute-start(bf16[128,1024]{1,0:T(8,128)(2,1)S(1)} %copy-done.24), channel_id=1, source_target_pairs={{0,2},{2,0},{4,6},{6,4},{8,10},{10,8},{12,14},{14,12},{16,18},{18,... | collective-permute-start | bytes 786440 | tf_op jit(solution)/shard_map/ppermute | solution.py:338
  157.7 9.1 %collective-permute-start.20 = (bf16[128,1024]{1,0:T(8,128)(2,1)S(1)}, bf16[128,1024]{1,0:T(8,128)(2,1)S(1)}, u32[]{:S(2)}, u32[]{:S(2)}) collective-permute-start(bf16[128,1024]{1,0:T(8,128)(2,1)S(1)} %copy-done.23), channel_id=1, source_target_pairs={{0,4},{2,6},{4,0},{6,2},{8,12},{10,14},{12,8},{14,10},{16,20},{18,... | collective-permute-start | bytes 786440 | tf_op jit(solution)/shard_map/ppermute | solution.py:338
  163.3 27.6 %collective-permute-start.10 = (bf16[144,1024]{1,0:T(8,128)(2,1)}, bf16[144,1024]{1,0:T(8,128)(2,1)S(1)}, u32[]{:S(2)}, u32[]{:S(2)}) collective-permute-start(bf16[144,1024]{1,0:T(8,128)(2,1)} %merge.5.refs_8_), channel_id=1, source_target_pairs={{0,2},{2,0},{4,6},{6,4},{8,10},{10,8},{12,14},{14,12},{16,18},{18,... | collective-permute-start | bytes 884744 | tf_op jit(solution)/shard_map/ppermute | solution.py:338
  164.6 26.3 %collective-permute-start.11 = (bf16[144,1024]{1,0:T(8,128)(2,1)}, bf16[144,1024]{1,0:T(8,128)(2,1)S(1)}, u32[]{:S(2)}, u32[]{:S(2)}) collective-permute-start(bf16[144,1024]{1,0:T(8,128)(2,1)} %merge.5.refs_8_), channel_id=1, source_target_pairs={{0,4},{2,6},{4,0},{6,2},{8,12},{10,14},{12,8},{14,10},{16,20},{18,... | collective-permute-start | bytes 884744 | tf_op jit(solution)/shard_map/ppermute | solution.py:338
  165.3 25.6 %collective-permute-start.12 = (bf16[144,1024]{1,0:T(8,128)(2,1)}, bf16[144,1024]{1,0:T(8,128)(2,1)S(1)}, u32[]{:S(2)}, u32[]{:S(2)}) collective-permute-start(bf16[144,1024]{1,0:T(8,128)(2,1)} %merge.5.refs_8_), channel_id=1, source_target_pairs={{0,6},{2,4},{4,2},{6,0},{8,14},{10,12},{12,10},{14,8},{16,22},{18,... | collective-permute-start | bytes 884744 | tf_op jit(solution)/shard_map/ppermute | solution.py:338
  166.8 14.5 %collective-permute-start.21 = (bf16[128,1024]{1,0:T(8,128)(2,1)S(1)}, bf16[128,1024]{1,0:T(8,128)(2,1)S(1)}, u32[]{:S(2)}, u32[]{:S(2)}) collective-permute-start(bf16[128,1024]{1,0:T(8,128)(2,1)S(1)} %copy-done.22), channel_id=1, source_target_pairs={{0,6},{2,4},{4,2},{6,0},{8,14},{10,12},{12,10},{14,8},{16,22},{18,... | collective-permute-start | bytes 786440 | tf_op jit(solution)/shard_map/ppermute | solution.py:338
  184.1 36.2 %collective-permute-start.22 = (bf16[144,1024]{1,0:T(8,128)(2,1)}, bf16[144,1024]{1,0:T(8,128)(2,1)S(1)}, u32[]{:S(2)}, u32[]{:S(2)}) collective-permute-start(bf16[144,1024]{1,0:T(8,128)(2,1)} %message.3.refs_0_), channel_id=1, source_target_pairs={{0,8},{2,10},{4,12},{6,14},{8,16},{10,18},{12,20},{14,22},{16,24},... | collective-permute-start | bytes 884744 | tf_op jit(solution)/shard_map/ppermute | solution.py:341
  213.3 50.3 %collective-permute-start.14 = (bf16[1024,768]{1,0:T(8,128)(2,1)}, bf16[1024,768]{1,0:T(8,128)(2,1)S(1)}, u32[]{:S(2)}, u32[]{:S(2)}) collective-permute-start(bf16[1024,768]{1,0:T(8,128)(2,1)} %get-tuple-element.96), channel_id=1, source_target_pairs={{0,1},{1,0},{2,3},{3,2},{4,5},{5,4},{6,7},{7,6},{8,9},{9,8},{10,11... | collective-permute-start | bytes 4718600 | tf_op jit(solution)/shard_map/ppermute | solution.py:518
  219.7 35.9 %collective-permute-start.18 = (bf16[1024,256]{1,0:T(8,128)(2,1)S(1)}, bf16[1024,256]{1,0:T(8,128)(2,1)S(1)}, u32[]{:S(2)}, u32[]{:S(2)}) collective-permute-start(bf16[1024,256]{1,0:T(8,128)(2,1)S(1)} %convolution_convert_fusion), channel_id=1, source_target_pairs={{0,1},{1,0},{2,3},{3,2},{4,5},{5,4},{6,7},{7,6},{8,9},{9,8},{10,11... | collective-permute-start | bytes 1572872 | tf_op jit(solution)/shard_map/ppermute | solution.py:518
  222.9 24.9 %collective-permute-start.23 = (bf16[144,1024]{1,0:T(8,128)(2,1)}, bf16[144,1024]{1,0:T(8,128)(2,1)S(1)}, u32[]{:S(2)}, u32[]{:S(2)}) collective-permute-start(bf16[144,1024]{1,0:T(8,128)(2,1)} %merge.6), channel_id=1, source_target_pairs={{0,16},{2,18},{4,20},{6,22},{8,24},{10,26},{12,28},{14,30},{1,17},... | collective-permute-start | bytes 884744 | tf_op jit(solution)/shard_map/ppermute | solution.py:341
  255.8 6.1 %collective-permute-start.29 = (bf16[256,128]{1,0:T(8,128)(2,1)}, bf16[256,128]{1,0:T(8,128)(2,1)S(1)}, u32[]{:S(2)}, u32[]{:S(2)}) collective-permute-start(bf16[256,128]{1,0:T(8,128)(2,1)} %get-tuple-element.117), channel_id=1, source_target_pairs={{0,6},{2,4},{4,2},{6,0},{8,14},{10,12},{12,10},{14,8},{16,22},{18,... | collective-permute-start | bytes 196616 | tf_op jit(solution)/shard_map/ppermute | solution.py:338
  257.3 5.3 %collective-permute-start.28 = (bf16[256,128]{1,0:T(8,128)(2,1)}, bf16[256,128]{1,0:T(8,128)(2,1)S(1)}, u32[]{:S(2)}, u32[]{:S(2)}) collective-permute-start(bf16[256,128]{1,0:T(8,128)(2,1)} %get-tuple-element.116), channel_id=1, source_target_pairs={{0,4},{2,6},{4,0},{6,2},{8,12},{10,14},{12,8},{14,10},{16,20},{18,... | collective-permute-start | bytes 196616 | tf_op jit(solution)/shard_map/ppermute | solution.py:338
  258.4 5.1 %collective-permute-start.27 = (bf16[256,128]{1,0:T(8,128)(2,1)}, bf16[256,128]{1,0:T(8,128)(2,1)S(1)}, u32[]{:S(2)}, u32[]{:S(2)}) collective-permute-start(bf16[256,128]{1,0:T(8,128)(2,1)} %get-tuple-element.115), channel_id=1, source_target_pairs={{0,2},{2,0},{4,6},{6,4},{8,10},{10,8},{12,14},{14,12},{16,18},{18,... | collective-permute-start | bytes 196616 | tf_op jit(solution)/shard_map/ppermute | solution.py:338
  259.3 8.5 %collective-permute-start.24 = (bf16[256,256]{1,0:T(8,128)(2,1)S(1)}, bf16[256,256]{1,0:T(8,128)(2,1)S(1)}, u32[]{:S(2)}, u32[]{:S(2)}) collective-permute-start(bf16[256,256]{1,0:T(8,128)(2,1)S(1)} %get-tuple-element.126), channel_id=1, source_target_pairs={{0,2},{2,0},{4,6},{6,4},{8,10},{10,8},{12,14},{14,12},{16,18},{18,... | collective-permute-start | bytes 393224 | tf_op jit(solution)/shard_map/ppermute | solution.py:338
  261.8 8.2 %collective-permute-start.25 = (bf16[256,256]{1,0:T(8,128)(2,1)S(1)}, bf16[256,256]{1,0:T(8,128)(2,1)S(1)}, u32[]{:S(2)}, u32[]{:S(2)}) collective-permute-start(bf16[256,256]{1,0:T(8,128)(2,1)S(1)} %get-tuple-element.125), channel_id=1, source_target_pairs={{0,4},{2,6},{4,0},{6,2},{8,12},{10,14},{12,8},{14,10},{16,20},{18,... | collective-permute-start | bytes 393224 | tf_op jit(solution)/shard_map/ppermute | solution.py:338
  263.6 2.8 collective-permute-start.30
  264.2 23.4 %collective-permute-start.15 = (bf16[256,768]{1,0:T(8,128)(2,1)S(1)}, bf16[256,768]{1,0:T(8,128)(2,1)S(1)}, u32[]{:S(2)}, u32[]{:S(2)}) collective-permute-start(bf16[256,768]{1,0:T(8,128)(2,1)S(1)} %get-tuple-element.122), channel_id=1, source_target_pairs={{0,2},{2,0},{4,6},{6,4},{8,10},{10,8},{12,14},{14,12},{16,18},{18,... | collective-permute-start | bytes 1179656 | tf_op jit(solution)/shard_map/ppermute | solution.py:338
  265.4 22.5 %collective-permute-start.16 = (bf16[256,768]{1,0:T(8,128)(2,1)S(1)}, bf16[256,768]{1,0:T(8,128)(2,1)S(1)}, u32[]{:S(2)}, u32[]{:S(2)}) collective-permute-start(bf16[256,768]{1,0:T(8,128)(2,1)S(1)} %get-tuple-element.121), channel_id=1, source_target_pairs={{0,4},{2,6},{4,0},{6,2},{8,12},{10,14},{12,8},{14,10},{16,20},{18,... | collective-permute-start | bytes 1179656 | tf_op jit(solution)/shard_map/ppermute | solution.py:338
  266.3 21.5 %collective-permute-start.17 = (bf16[256,768]{1,0:T(8,128)(2,1)S(1)}, bf16[256,768]{1,0:T(8,128)(2,1)S(1)}, u32[]{:S(2)}, u32[]{:S(2)}) collective-permute-start(bf16[256,768]{1,0:T(8,128)(2,1)S(1)} %get-tuple-element.120), channel_id=1, source_target_pairs={{0,6},{2,4},{4,2},{6,0},{8,14},{10,12},{12,10},{14,8},{16,22},{18,... | collective-permute-start | bytes 1179656 | tf_op jit(solution)/shard_map/ppermute | solution.py:338
  267.8 19.8 %collective-permute-start.26 = (bf16[256,256]{1,0:T(8,128)(2,1)S(1)}, bf16[256,256]{1,0:T(8,128)(2,1)S(1)}, u32[]{:S(2)}, u32[]{:S(2)}) collective-permute-start(bf16[256,256]{1,0:T(8,128)(2,1)S(1)} %get-tuple-element.124), channel_id=1, source_target_pairs={{0,6},{2,4},{4,2},{6,0},{8,14},{10,12},{12,10},{14,8},{16,22},{18,... | collective-permute-start | bytes 393224 | tf_op jit(solution)/shard_map/ppermute | solution.py:338
  (24 other events, 229.8 us)

commit v3 on v2

--- a/solution.py
+++ b/solution.py
@@ -67,8 +67,51 @@
         each(h, jnp.exp(jnp.where(later, log, -jnp.inf)))
 
 
-def own_kernel(n_heads, at, x, top, bottom, b, c, log_top, log_bottom, *refs):
-    ends, (write_local, read_local, total, cum, cum_t) = refs[:RING], refs[RING:]
+def own_logs(log_decay):
+    rows, n_heads = log_decay.shape
+    return jnp.concatenate([log_decay[...], jnp.zeros((rows, LANES - n_heads), f32)], axis=1)
+
+
+def edge_kernel(n_heads, at, x, dy, b, c, log_decay, *refs):
+    messages, cum = refs[:RING], refs[RING]
+    g = pl.program_id(0)
+    heads = n_heads // RING
+    rows = x.shape[0]
+    width = x.shape[1] // heads
+    n = b.shape[1]
+
+    @pl.when(g == 0)
+    def _():
+        upto = (iota((rows, rows), 0) <= iota((rows, rows), 1)).astype(f32)
+        cum[...] = mm_exact(upto, own_logs(log_decay), TN)
+
+    col = group_of(cum[...], g, heads, 1)
+    last = col[rows - 1 : rows, :]
+    tailed = (x[...].astype(f32) * spread(jnp.exp(last - col), width)).astype(bf16)
+    decayed = (dy[...].astype(f32) * spread(jnp.exp(col), width)).astype(bf16)
+    ends = mm(b[...], tailed, TN).astype(bf16)
+    fronts = mm(c[...], decayed, TN).astype(bf16)
+    log = spread(last, width)
+    for j in range(RING):
+
+        @pl.when(lax.bitwise_xor(at[0], g) == j)
+        def _():
+            messages[j][:n] = ends
+            messages[j][n : 2 * n] = fronts
+            write_log(messages[j], log)
+
+
+def pack_kernel(n_heads, dy, b, c, log_decay, out):
+    rows, columns = dy.shape
+    parts = [v.astype(bf16) for v in three_parts(log_decay[...])]
+    fill = jnp.zeros((rows, LANES - 3 * n_heads), bf16)
+    out[:, :columns] = dy[...]
+    out[:, columns : columns + LANES] = b[...]
+    out[:, columns + LANES : columns + 2 * LANES] = c[...]
+    out[:, columns + 2 * LANES :] = jnp.concatenate(parts + [fill], axis=1)
+
+
+def own_kernel(n_heads, x, dy, b, c, log_decay, write_local, read_local, total, cum, cum_t):
     g = pl.program_id(0)
     heads = n_heads // RING
     rows = x.shape[0]
@@ -78,31 +121,26 @@
     @pl.when(g == 0)
     def _():
         total[...] = jnp.zeros_like(total)
-        cumulate(n_heads, (log_top, log_bottom), cum, cum_t)
+        logs = own_logs(log_decay)
+        upto = (iota((rows, rows), 0) <= iota((rows, rows), 1)).astype(f32)
+        cum[...] = mm_exact(upto, logs, TN)
+        cum_t[...] = mm_exact(logs, upto, TN)
 
     col, row = group_of(cum[...], g, heads, 1), group_of(cum_t[...], g, heads, 0)
-    mid, last = col[half - 1 : half, :], col[rows - 1 : rows, :]
-    for i, dy in enumerate((top, bottom)):
+    mid = col[half - 1 : half, :]
+    for i in range(2):
         lo = i * half
         parts = []
 
         def add(h, decay):
             span = slice(h * width, (h + 1) * width)
-            parts.append(decay * mm(x[lo : lo + half, span], dy[:, span], NT))
+            parts.append(decay * mm(x[lo : lo + half, span], dy[lo : lo + half, span], NT))
 
         diagonal(heads, half, lo, col, row, add)
         total[lo : lo + half, lo : lo + half] += sum(parts)
-    xf = x[...].astype(f32)
-    early = (xf[:half] * spread(jnp.exp(mid - col[:half]), width)).astype(bf16)
-    late = (bottom[...].astype(f32) * spread(jnp.exp(col[half:] - mid), width)).astype(bf16)
+    early = (x[:half].astype(f32) * spread(jnp.exp(mid - col[:half]), width)).astype(bf16)
+    late = (dy[half:].astype(f32) * spread(jnp.exp(col[half:] - mid), width)).astype(bf16)
     total[:half, half:] += mm(early, late, NT)
-    tailed = (xf * spread(jnp.exp(last - col), width)).astype(bf16)
-    mine = mm(b[...], tailed, TN).astype(bf16)
-    for j in range(RING):
-
-        @pl.when(lax.bitwise_xor(at[0], g) == j)
-        def _():
-            ends[j][...] = mine
 
     @pl.when(g == pl.num_programs(0) - 1)
     def _():
@@ -156,21 +194,19 @@
     return total
 
 
-def combine_kernel(way, at, *refs):
-    parts, logs, out = refs[:RING], [r[...] for r in refs[RING : 2 * RING]], refs[2 * RING]
+def combine_kernel(at, *refs):
+    parts, (state_out, grad_out) = refs[:RING], refs[RING:]
+    n = state_out.shape[0] - EXTRA
+    logs = [log_of(part) for part in parts]
     p = at[0]
-    n = out.shape[0] - EXTRA
-    total = 0.0
+    state, grad = 0.0, 0.0
     for j in range(RING):
         own = lax.bitwise_xor(p, j)
-        if way == 1:
-            weight = jnp.exp(log_over(p, logs, lambda k: k > own))
-        else:
-            weight = jnp.exp(log_over(p, logs, lambda k: k < own))
-        part = parts[j][0] if len(parts[j].shape) == 3 else parts[j][...]
-        total += part.astype(f32) * weight
-    out[:n] = total.astype(bf16)
-    write_log(out, sum(logs))
+        state += parts[j][:n].astype(f32) * jnp.exp(log_over(p, logs, lambda k: k > own))
+        grad += parts[j][n : 2 * n].astype(f32) * jnp.exp(log_over(p, logs, lambda k: k < own))
+    for out, value in ((state_out, state), (grad_out, grad)):
+        out[:n] = value.astype(bf16)
+        write_log(out, sum(logs))
 
 
 def write_log(out, log):
@@ -188,11 +224,12 @@
     return tail[0:1] + tail[1:2] + tail[2:3]
 
 
-def merge_kernel(near, far, out):
-    n = near.shape[0] - EXTRA
-    log = log_of(near)
-    out[:n] = (near[:n].astype(f32) + far[:n].astype(f32) * jnp.exp(log)).astype(bf16)
-    write_log(out, log + log_of(far))
+def merge_kernel(*refs):
+    for near, far, out in ((*refs[:2], refs[4]), (*refs[2:4], refs[5])):
+        n = near.shape[0] - EXTRA
+        log = log_of(near)
+        out[:n] = (near[:n].astype(f32) + far[:n].astype(f32) * jnp.exp(log)).astype(bf16)
+        write_log(out, log + log_of(far))
 
 
 def ring_kernel(at, *refs):
@@ -209,7 +246,7 @@
         outs[j][0] = total.astype(bf16)
 
 
-def finish_kernel(n_heads, n_w, at, *refs):
+def finish_kernel(n_heads, n_w, outer, share, at, *refs):
     locals_, refs = refs[:RING], refs[RING:]
     rings, refs = refs[:RING], refs[RING:]
     quarters, refs = refs[:RING], refs[RING:]
@@ -218,7 +255,7 @@
     bottoms, refs = refs[:RING], refs[RING:]
     cums, refs = refs[:RING], refs[RING:]
     w, refs = refs[:n_w], refs[n_w:]
-    x, acts, own, write, tiles, total = refs
+    x, acts, own, write, *tiles, total = refs
     g, p = pl.program_id(0), at[0]
     heads = n_heads // RING
     rows = own.shape[0]
@@ -253,15 +290,34 @@
 
     @pl.when(g == pl.num_programs(0) - 1)
     def _():
-        tiles[...] = total[...].astype(tiles.dtype)
+        if len(tiles) == 1:
+            for k in range(n_w):
+                put_tile(tiles[0], lax.rem(at[1] + k, outer), total, k, n_rows)
+        else:
+            for tile in tiles:
+                tile[...] = jnp.zeros_like(tile)
+            for k in range(n_w):
+                o = lax.rem(at[1] + k, outer)
+                for tile, side in zip(tiles, (at[2], 1 - at[2])):
+
+                    @pl.when(lax.div(o, share) == side)
+                    def _():
+                        put_tile(tile, lax.rem(o, share), total, k, n_rows)
+
+
+def put_tile(tile, slot, total, k, n_rows):
+    rows = total.shape[0] // RING
+    for j in range(RING):
+        part = total[j * rows : (j + 1) * rows, k * n_rows : (k + 1) * n_rows]
+        tile[j, slot] = part.astype(tile.dtype)
 
 
 def read_kernel(n_heads, at, *refs):
     tops, refs = refs[:RING], refs[RING:]
     bottoms, refs = refs[:RING], refs[RING:]
     cums, refs = refs[:RING], refs[RING:]
-    logs, refs = [r[...] for r in refs[:RING]], refs[RING:]
-    ends, (carried, *outs) = refs[:RING], refs[RING:]
+    parts, (carried, *outs) = refs[:RING], refs[RING:]
+    logs = [log_of(part) for part in parts]
     p = at[0]
     heads = n_heads // RING
     half = tops[0].shape[0]
@@ -274,7 +330,7 @@
             if i != j:
                 there = lax.bitwise_xor(p, i)
                 weight = jnp.exp(log_over(p, logs, lambda k: (k < own) & (k > there)))
-                total += ends[i][...].astype(f32) * jnp.where(there < own, weight, 0.0)
+                total += parts[i][:n].astype(f32) * jnp.where(there < own, weight, 0.0)
         states = total.astype(bf16)
         decay = spread(jnp.exp(group_of(cums[j][...], p, heads, 1)), width)
         for i, dy in enumerate((tops[j], bottoms[j])):
@@ -284,21 +340,21 @@
 
 
 def place_kernel(outer, share, at, *refs):
-    blocks, out = refs[:-1], refs[-1]
+    blocks, late, out = refs[:RING], refs[RING:-1], refs[-1]
     p, z, side = at[0], at[1], at[2]
     width = out.shape[1] // (share * RING)
-    for k in range(outer):
-        o = lax.rem(z + k, outer)
-        first = lax.rem(o, share) * RING
-
-        @pl.when(lax.div(o, share) == side)
-        def _():
-            for j in range(RING):
-                column = pl.multiple_of((first + lax.bitwise_xor(p, j)) * width, width)
-                if k < outer - 1:
-                    out[:, pl.ds(column, width)] = blocks[j][:, k * width : (k + 1) * width]
-                else:
-                    out[:, pl.ds(column, width)] = blocks[RING + j][...]
+    last = lax.rem(z + outer - 1, outer)
+    for slot in range(share):
+        for j in range(RING):
+            column = pl.multiple_of((slot * RING + lax.bitwise_xor(p, j)) * width, width)
+
+            @pl.when(side * share + slot == last)
+            def _():
+                out[:, pl.ds(column, width)] = late[j][...]
+
+            @pl.when(side * share + slot != last)
+            def _():
+                out[:, pl.ds(column, width)] = blocks[j][slot]
 
 
 def call(kernel, name, grid, in_specs, out_specs, out_shape, scratch=(), prefetch=1):
@@ -332,7 +388,7 @@
     place = lax.axis_index("seq")
     side = lax.axis_index("head")
     p, z = place % RING, place // RING
-    at = p.astype(jnp.int32)[None]
+    at = jnp.stack([p, z, side]).astype(jnp.int32)
 
     def swap(value, j):
         return lax.ppermute(value, "seq", [(s, s ^ j) for s in range(n_seq)])
@@ -349,29 +405,6 @@
         w_blocks.append(lax.ppermute(w_blocks[-1], "seq", turn))
 
     turn_w()
-
-    first = lax.reduce_precision(log_decay, 8, 7)
-    second = lax.reduce_precision(log_decay - first, 8, 7)
-    third = log_decay - first - second
-    fill = jnp.zeros((rows, LANES - 3 * n_heads), bf16)
-    beside = [write_proj, read_proj] + [v.astype(bf16) for v in (first, second, third)] + [fill]
-    own_top = jnp.concatenate([v[:half] for v in [dy] + beside], axis=1)
-    own_bottom = jnp.concatenate([v[half:] for v in [dy] + beside], axis=1)
-    x_top, y_bottom = swap(own_top, 1), swap(own_bottom, 2)
-    x_bottom, y_top = swap(own_bottom, 1), swap(own_top, 2)
-    x_top, x_bottom, y_top, y_bottom = lax.optimization_barrier((x_top, x_bottom, y_top, y_bottom))
-    blocks = [
-        (own_top, own_bottom),
-        (x_top, x_bottom),
-        (y_top, y_bottom),
-        (swap(x_top, 2), swap(y_bottom, 1)),
-    ]
-
-    half_spec = pl.BlockSpec((half, part), lambda g, q: (0, g))
-    first_tile = columns // LANES
-
-    def tile_spec(i):
-        return pl.BlockSpec((half, LANES), lambda g, q: (0, first_tile + i))
 
     def const(*shape):
         return pl.BlockSpec(shape, lambda g, q: (0,) * len(shape))
@@ -389,84 +422,114 @@
     message_shape = shape((state_dim + EXTRA, part), bf16)
     cum_scratch, cum_t_scratch = pltpu.VMEM((rows, LANES), f32), pltpu.VMEM((LANES, rows), f32)
 
-    *ends, write_local, read_local = call(
-        functools.partial(own_kernel, n_heads),
+    log_in_spec = const(rows, n_heads)
+    own_specs = [by_group, by_group, proj_spec, proj_spec, log_in_spec]
+    part_spec = const(2 * state_dim + EXTRA, part)
+    parts = call(
+        functools.partial(edge_kernel, n_heads),
+        "edges",
+        (RING,),
+        own_specs,
+        [part_spec] * RING,
+        [shape((2 * state_dim + EXTRA, part), bf16)] * RING,
+        [cum_scratch],
+    )(at, x, dy, write_proj, read_proj, log_decay)
+    parts = [parts[0]] + [swap(parts[j], j) for j in range(1, RING)]
+
+    write_local, read_local = call(
+        functools.partial(lambda *refs: own_kernel(n_heads, *refs[1:])),
         "own_tokens",
         (RING,),
-        [by_group, half_spec, half_spec, proj_spec, proj_spec, tile_spec(2), tile_spec(2)],
-        [const(state_dim, part)] * RING + [proj_spec] * 2,
-        [shape((state_dim, part), bf16)] * RING + [shape((rows, state_dim), f32)] * 2,
+        own_specs,
+        [proj_spec] * 2,
+        [shape((rows, state_dim), f32)] * 2,
         [pltpu.VMEM((rows, rows), f32), cum_scratch, cum_t_scratch],
-    )(at, x, own_top, own_bottom, write_proj, read_proj, own_top, own_bottom)
-
-    def block(j):
-        top, bottom = blocks[j]
+    )(at, x, dy, write_proj, read_proj, log_decay)
+
+    packed = call(
+        functools.partial(lambda *refs: pack_kernel(n_heads, *refs[1:])),
+        "pack",
+        (1,),
+        [const(rows, columns), proj_spec, proj_spec, log_in_spec],
+        const(rows, columns + 3 * LANES),
+        shape((rows, columns + 3 * LANES), bf16),
+    )(at, dy, write_proj, read_proj, log_decay)
+
+    def halves(width, column):
+        upper = pl.BlockSpec((half, width), lambda g, q: (0, column(g, q)))
+        lower = pl.BlockSpec((half, width), lambda g, q: (1, column(g, q)))
+        return [(upper, lower)] * (RING - 1) + [(upper, upper)]
+
+    half_specs = halves(part, lambda g, q: g)
+    mine_specs = halves(part, lambda g, q: q[0])
+    tile_specs = [halves(LANES, lambda g, q, i=i: columns // LANES + i) for i in range(3)]
+
+    def block(j, top, bottom):
         return call(
             functools.partial(lambda *refs: block_kernel(n_heads, *refs[1:])),
             "tokens",
             (RING,),
-            [half_spec, half_spec] + [tile_spec(i) for i in range(3) for _ in range(2)],
+            [*half_specs[j]] + [spec for specs in tile_specs for spec in specs[j]],
             [by_group, state_spec, log_spec, cum_spec],
             [shape((rows, columns), bf16), state_shape, log_shape, cum_shape],
             [cum_t_scratch],
         )(at, top, bottom, *([top, bottom] * 3))
 
-    results = [block(0)]
+    results = [block(0, packed, packed)]
     logs = [results[0][2]]
-    logs[0], read_local, w_blocks[-1] = lax.optimization_barrier(
-        (logs[0], read_local, w_blocks[-1])
-    )
-    results += [block(j) for j in range(1, RING - 1)]
-    logs += [v[2] for v in results[1:]]
-    logs, blocks[-1] = lax.optimization_barrier((logs, blocks[-1]))
-    results.append(block(RING - 1))
-    logs.append(results[-1][2])
-    local_acts, fronts, _, cums = zip(*results)
-
-    mine3 = pl.BlockSpec((1, state_dim, part), lambda g, q: (q[0], 0, 0))
-    mine_log = pl.BlockSpec((1, part), lambda g, q: (0, q[0]))
-
-    def combine(parts, way):
+    packed, parts, logs, read_local = lax.optimization_barrier((packed, parts, logs, read_local))
+    from_x, from_y = lax.optimization_barrier((swap(packed, 1), swap(packed, 2)))
+
+    def combine():
         return call(
-            functools.partial(combine_kernel, way),
-            "message",
+            combine_kernel,
+            "messages",
             (1,),
-            [mine3 if v.ndim == 3 else const(*v.shape) for v in parts] + [mine_log] * RING,
-            message_spec,
-            message_shape,
-        )(at, *parts, *logs)
-
-    def merge(near, far):
+            [part_spec] * RING,
+            [message_spec] * 2,
+            [message_shape] * 2,
+        )(at, *parts)
+
+    def merge(*pairs):
         return call(
             lambda q, *refs: merge_kernel(*refs),
             "merge",
             (1,),
+            [message_spec] * 4,
             [message_spec] * 2,
-            message_spec,
-            message_shape,
-        )(at, near, far)
-
+            [message_shape] * 2,
+        )(at, *pairs)
+
+    state_span, grad_span = combine()
+    d = 1
+    while d < outer:
+        state_got, grad_got = along(state_span, d), along(grad_span, -d)
+        if d == 1:
+            state_part, grad_part = state_got, grad_got
+        else:
+            state_part, grad_part = merge(state_part, state_got, grad_part, grad_got)
+        if 2 * d < outer:
+            state_span, grad_span = merge(state_span, state_got, grad_span, grad_got)
+        d *= 2
+    state_got, grad_got, w_blocks[-1] = lax.optimization_barrier(
+        (state_got, grad_got, w_blocks[-1])
+    )
+    turn_w()
+    grad_parts = [grad_part] + [swap(grad_part, j) for j in range(1, RING)]
+
+    blocks = [(packed, packed), (from_x, from_x), (from_y, from_y)]
+    blocks.append((swap(from_x[:half], 2), swap(from_y[half:], 1)))
+    results += [block(j, *blocks[j]) for j in range(1, RING - 1)]
+    logs += [v[2] for v in results[1:]]
+    logs, blocks[-1] = lax.optimization_barrier((logs, blocks[-1]))
+    results.append(block(RING - 1, *blocks[-1]))
+    logs.append(results[-1][2])
+    local_acts, fronts, _, cums = zip(*results)
     fronts = list(fronts)
-    while len(w_blocks) < min(3, outer):
-        turn_w()
-    fronts[-1], w_blocks[-1] = lax.optimization_barrier((fronts[-1], w_blocks[-1]))
+    if outer > 2:
+        fronts[-1], w_blocks[-1] = lax.optimization_barrier((fronts[-1], w_blocks[-1]))
     while len(w_blocks) < outer:
         turn_w()
-
-    def scan_along(span, way, after=None):
-        result, d = None, 1
-        while d < outer:
-            got = along(span, way * d)
-            if after is not None:
-                got = after(got)
-            result = got if result is None else merge(result, got)
-            if 2 * d < outer:
-                span = merge(span, got)
-            d *= 2
-        return result
-
-    grad_part = scan_along(combine(fronts, -1), -1)
-    grad_parts = [grad_part] + [swap(grad_part, j) for j in range(1, RING)]
 
     ring_grads = call(
         ring_kernel,
@@ -477,28 +540,32 @@
         [state_shape] * RING,
     )(at, *fronts, *logs)
 
-    n_w = outer - 1
+    two = n_head == 2 and w_rows % LANES == 0
+    share = outer // n_head
+    n_w = outer - 1 if two else outer
     tall = pl.BlockSpec((RING * rows, part), lambda g, q: (0, g))
     w_spec = pl.BlockSpec((w_rows, part), lambda g, q: (0, g))
-    acts, act_grad, write_carry, tiles = call(
-        functools.partial(finish_kernel, n_heads, n_w),
+    tile_shapes = [(RING, share, rows, w_rows)] * 2 if two else [(RING, outer, rows, w_rows)]
+    acts, act_grad, write_carry, *tiles = call(
+        functools.partial(finish_kernel, n_heads, n_w, outer, share),
         "finish",
         (RING,),
         [by_group] * RING
         + [state_spec] * RING
         + [message_spec] * RING
         + [log_spec] * RING
-        + [tile_spec(0)] * (2 * RING)
+        + [spec[0] for spec in tile_specs[0]]
+        + [spec[1] for spec in tile_specs[0]]
         + [cum_spec] * RING
         + [w_spec] * n_w
         + [by_group],
-        [tall, by_group, proj_spec, const(RING * rows, n_w * w_rows)],
+        [tall, by_group, proj_spec] + [const(*v) for v in tile_shapes],
         [
             shape((RING * rows, columns), bf16),
             shape((rows, columns), bf16),
             shape((rows, state_dim), f32),
-            shape((RING * rows, n_w * w_rows), bf16),
-        ],
+        ]
+        + [shape(v, bf16) for v in tile_shapes],
         [pltpu.VMEM((RING * rows, n_w * w_rows), f32)],
     )(
         at,
@@ -513,39 +580,13 @@
         x,
     )
 
-    def over_head(tile):
-        if n_head == 2:
-            got = lax.ppermute(tile, "head", [(0, 1), (1, 0)])
-            return (tile.astype(f32) + got.astype(f32)).astype(bf16)
-        return lax.psum(tile.astype(f32), "head").astype(bf16)
-
-    def to_owners(tile):
-        return [tile[:rows]] + [swap(tile[j * rows : (j + 1) * rows], j) for j in range(1, RING)]
-
-    share = outer // n_head
-    tiles, w_blocks[-1] = lax.optimization_barrier((tiles, w_blocks[-1]))
-    early = over_head(tiles)
-    late_tile = mm(acts, w_blocks[-1], NT).astype(bf16)
-
-    held = [tiles, late_tile]
-
-    def after(got):
-        held[0], got = lax.optimization_barrier((held[0], got))
-        held[0] = held[1]
-        return got
-
-    my_ends = [ends[0]] + [swap(ends[j], j) for j in range(1, RING)]
-    state_part = scan_along(combine(my_ends, 1), 1, after)
-    mine_half = pl.BlockSpec((half, part), lambda g, q: (0, q[0]))
     read_parts = call(
         functools.partial(read_kernel, n_heads),
         "read_carry",
         (1,),
-        [mine_half] * (2 * RING)
-        + [cum_spec] * RING
-        + [mine_log] * RING
-        + [const(state_dim, part)] * RING
-        + [message_spec],
+        [spec[0] for spec in mine_specs]
+        + [spec[1] for spec in mine_specs]
+        + [cum_spec] * RING + [part_spec] * RING + [message_spec],
         [proj_spec] * RING,
         [shape((rows, state_dim), bf16)] * RING,
     )(
@@ -553,15 +594,9 @@
         *[top for top, _ in blocks],
         *[bottom for _, bottom in blocks],
         *cums,
-        *logs,
-        *my_ends,
+        *parts,
         state_part,
     )
-
-    late = over_head(late_tile)
-    late, read_parts = lax.optimization_barrier((late, read_parts))
-    late = to_owners(late)
-    early = to_owners(early)
     read_carry = read_parts[0].astype(f32) + sum(
         swap(read_parts[j], j).astype(f32) for j in range(1, RING)
     )
@@ -571,7 +606,33 @@
     else:
         both = lax.psum(both, "head")
 
-    if w_rows % LANES == 0:
+    def to_owners(tile):
+        return [tile[0]] + [swap(tile[j], j) for j in range(1, RING)]
+
+    if two:
+        mine, theirs = tiles
+        got = lax.ppermute(theirs, "head", [(0, 1), (1, 0)])
+        early = (mine.astype(f32) + got.astype(f32)).astype(bf16)
+        _, w_last = lax.optimization_barrier((early, w_blocks[-1]))
+        tile = mm(acts, w_last, NT).astype(bf16)
+
+        def owner(s):
+            return (s // RING + outer - 1) % outer // share
+
+        both_axes = ("seq", "head")
+        got = lax.ppermute(
+            tile, both_axes, [(2 * s + 1 - owner(s), 2 * s + owner(s)) for s in range(n_seq)]
+        )
+        tile = (tile.astype(f32) + got.astype(f32)).astype(bf16).reshape(RING, rows, w_rows)
+        late = [tile[0]] + [
+            lax.ppermute(
+                tile[j],
+                both_axes,
+                [(2 * s + owner(s), 2 * (s ^ j) + owner(s)) for s in range(n_seq)],
+            )
+            for j in range(1, RING)
+        ]
+        early = to_owners(early)
         input_grad = pl.pallas_call(
             functools.partial(place_kernel, outer, share),
             in_specs=[pl.BlockSpec(memory_space=pltpu.SMEM)]
@@ -580,13 +641,11 @@
             out_shape=shape((rows, share * RING * w_rows), bf16),
             compiler_params=pltpu.CompilerParams(vmem_limit_bytes=32 * 2**20),
             name="place",
-        )(jnp.stack([p, z, side]).astype(jnp.int32), *early, *late)
+        )(at, *early, *late)
     else:
-        order = p ^ jnp.arange(RING)
-        pieces = jnp.concatenate([jnp.stack(early), jnp.stack(late)], axis=2)
-        pieces = jnp.take(pieces.reshape(RING, rows, outer, w_rows), order, axis=0)
-        pieces = jnp.take(pieces, (side * share + jnp.arange(share) - z) % outer, axis=2)
-        input_grad = pieces.transpose(1, 2, 0, 3).reshape(rows, share * RING * w_rows)
+        summed = lax.psum_scatter(tiles[0], "head", scatter_dimension=1, tiled=True)
+        pieces = jnp.take(jnp.stack(to_owners(summed)), p ^ jnp.arange(RING), axis=0)
+        input_grad = pieces.transpose(2, 1, 0, 3).reshape(rows, share * RING * w_rows)
     return (input_grad, act_grad, both[0], both[1])
 
 

time: 291 us -> 218 us (0.75)
  the two profiles are of different devices: /device:TPU:24 before, /device:TPU:1 now
where the time goes in v3:
time: 218 us; the launch traced here: 217 us
  Pallas kernels  96.8 us (44%)
  waiting for transfers between devices  52.7 us (24%)
  starting transfers between devices  51.5 us (24%)
  local copies, waits for them, and re-layouts  7.3 us (3%)
  matrix products  5.75 us (3%)
    pallas_call x4, Pallas kernels, block(): call(functools.partial(lambda *refs: block_kernel(n_heads, *refs[1:])), '...  32 us
    ppermute x16, waiting for transfers between devices, swap(): return lax.ppermute(value, 'seq', [(s, s ^ j) for s in range(n_seq)])  29.5 us
    pallas_call x1, Pallas kernels, local(): call(functools.partial(finish_kernel, n_heads, n_w, outer, share), 'finis...  21.1 us
    ppermute x4, waiting for transfers between devices, along(): lax.ppermute(value, 'seq', [(s, s + d * RING) for s in range(n_seq) if 0...  17.4 us
    ppermute x3, starting transfers between devices, turn_w(): w_blocks.append(lax.ppermute(w_blocks[-1], 'seq', turn))  14.7 us
    ppermute x16, starting transfers between devices, swap(): return lax.ppermute(value, 'seq', [(s, s ^ j) for s in range(n_seq)])  13.5 us
    ppermute x4, starting transfers between devices, along(): lax.ppermute(value, 'seq', [(s, s + d * RING) for s in range(n_seq) if 0...  9.11 us
    ppermute x3, starting transfers between devices, local(): lax.ppermute(tile[j], both_axes, [(2 * s + owner(s), 2 * (s ^ j) + owner(...  8.37 us
  transfers between devices with their start and end apart: 29, of which 16 were waited for; matrix products, arithmetic and copies ran while one was open for 5% of the time, Pallas kernels for 44%

profile of v3, /device:TPU:1, one launch (start us, length us, event | category | flops | bytes accessed | tf_op | source)
XLA Modules:
  0.0 216.9 jit_solution(14626728018289094442)
XLA Ops:
  0.6 4.2 %collective-permute-start.11 = (bf16[256,4096]{1,0:T(8,128)(2,1)}, bf16[256,4096]{1,0:T(8,128)(2,1)}, u32[]{:S(2)}, u32[]{:S(2)}) collective-permute-start(bf16[256,4096]{1,0:T(8,128)(2,1)} %refs_28_.1), channel_id=1, source_target_pairs={{0,24},{2,26},{4,28},{6,30},{8,0},{10,2},{12,4},{14,6},{16,8},{18,... | collective-permute-start | bytes 6291464 | tf_op jit(solution)/shard_map/ppermute | solution.py:405
  6.9 8.2 %edges.1 = (bf16[272,1024]{1,0:T(8,128)(2,1)}, bf16[272,1024]{1,0:T(8,128)(2,1)}, bf16[272,1024]{1,0:T(8,128)(2,1)}, bf16[272,1024]{1,0:T(8,128)(2,1)}) custom-call(s32[3]{0:T(128)} %pad_add_fusion.refs_0_.at.q, bf16[256,4096]{1,0:T(8,128)(2,1)} %refs_31_.1, bf16[256,4096]{1,0:T(8,128)(2,1)} %refs_2_.3, bf16[256,128]{1,0:T(8,128)(2,1)} %refs_3_.3, ...), custom_call_target="tpu_custom_call" | custom-call | tf_op jit(solution)/shard_map/edges/pallas_call | solution.py:428
  17.7 3.8 %pack.1.refs_1_.refs_2_.refs_3_.refs_4_.refs_5_.refs_6_.refs_7_.refs_8_.refs_16_.refs_20_.refs_0_ = bf16[256,4480]{1,0:T(8,128)(2,1)} custom-call(s32[3]{0:T(128)} %pad_add_fusion.refs_0_.at.q, bf16[256,4096]{1,0:T(8,128)(2,1)} %refs_2_.3, bf16[256,128]{1,0:T(8,128)(2,1)} %refs_3_.3, bf16[256,128]{1,0:T(8,128)(2,1)} %refs_4_.2, ...), custom_call_target="tpu_custom_call" | custom-call | tf_op jit(solution)/shard_map/pack/pallas_call | solution.py:449
  21.6 8.3 %own_tokens.1 = (f32[256,128]{1,0:T(8,128)}, f32[256,128]{1,0:T(8,128)}) custom-call(s32[3]{0:T(128)} %pad_add_fusion.refs_0_.at.q, bf16[256,4096]{1,0:T(8,128)(2,1)} %refs_31_.1, bf16[256,4096]{1,0:T(8,128)(2,1)} %refs_2_.3, bf16[256,128]{1,0:T(8,128)(2,1)} %refs_3_.3, bf16[256,128]{1,0:T(8,128)(2,1)} %refs_4_.2, f32[256,32]{1,0:T(8,128)} %copy.10.refs_4_.log_decay.refs_5_), custom_call_target="tpu_custom_call" | custom-call | tf_op jit(solution)/shard_map/own_tokens/pallas_call | solution.py:439
  29.9 8.1 %tokens.4 = (bf16[256,4096]{1,0:T(8,128)(2,1)}, bf16[4,128,1024]{2,1,0:T(8,128)(2,1)}, f32[1,4096]{1,0:T(1,128)}, f32[256,128]{1,0:T(8,128)}) custom-call(s32[3]{0:T(128)} %pad_add_fusion.refs_0_.at.q, bf16[256,4480]{1,0:T(8,128)(2,1)} %pack.1.refs_1_.refs_2_.refs_3_.refs_4_.refs_5_.refs_6_.refs_7_.refs_8_.refs_16_.refs_20_.refs_0_, ...), custom_call_target="tpu_custom_call" | custom-call | tf_op jit(solution)/shard_map/tokens/pallas_call | solution.py:468
  38.0 3.4 %collective-permute-done.2.refs_3_.refs_15_ = bf16[272,1024]{1,0:T(8,128)(2,1)S(1)} collective-permute-done((bf16[272,1024]{1,0:T(8,128)(2,1)}, bf16[272,1024]{1,0:T(8,128)(2,1)S(1)}, u32[]{:S(2)}, u32[]{:S(2)}) %collective-permute-start.2) | collective-permute-done | bytes 557088 | tf_op jit(solution)/shard_map/ppermute | solution.py:394
  43.7 3.4 %messages.1 = (bf16[144,1024]{1,0:T(8,128)(2,1)}, bf16[144,1024]{1,0:T(8,128)(2,1)}) custom-call(s32[3]{0:T(128)} %pad_add_fusion.refs_0_.at.q, bf16[272,1024]{1,0:T(8,128)(2,1)} %get-tuple-element.85.refs_0_.refs_12_, bf16[272,1024]{1,0:T(8,128)(2,1)} %copy-done.6, bf16[272,1024]{1,0:T(8,128)(2,1)} %copy-done.7, bf16[272,1024]{1,0:T(8,128)(2,1)} %copy-done.8), custom_call_target="tpu_custom_call" | custom-call | tf_op jit(solution)/shard_map/messages/pallas_call | solution.py:484
  49.7 5.7 %collective-permute-done.7.refs_1_.refs_0_ = bf16[144,1024]{1,0:T(8,128)(2,1)S(1)} collective-permute-done((bf16[144,1024]{1,0:T(8,128)(2,1)}, bf16[144,1024]{1,0:T(8,128)(2,1)S(1)}, u32[]{:S(2)}, u32[]{:S(2)}) %collective-permute-start.7) | collective-permute-done | bytes 294944 | tf_op jit(solution)/shard_map/ppermute | solution.py:397
  57.1 2.8 %merge.2 = (bf16[144,1024]{1,0:T(8,128)(2,1)}, bf16[144,1024]{1,0:T(8,128)(2,1)}) custom-call(s32[3]{0:T(128)} %pad_add_fusion.refs_0_.at.q, bf16[144,1024]{1,0:T(8,128)(2,1)} %get-tuple-element.89.refs_0_, bf16[144,1024]{1,0:T(8,128)(2,1)} %copy-done.9, bf16[144,1024]{1,0:T(8,128)(2,1)} %get-tuple-element.90.refs_2_, bf16[144,1024]{1,0:T(8,128)(2,1)} %copy-done.10), custom_call_target="tpu_custom_call" | custom-call | tf_op jit(solution)/shard_map/merge/pallas_call | solution.py:494
  61.2 5.2 %collective-permute-start.9 = (bf16[144,1024]{1,0:T(8,128)(2,1)}, bf16[144,1024]{1,0:T(8,128)(2,1)S(1)}, u32[]{:S(2)}, u32[]{:S(2)}) collective-permute-start(bf16[144,1024]{1,0:T(8,128)(2,1)} %get-tuple-element.91), channel_id=1, source_target_pairs={{0,16},{2,18},{4,20},{6,22},{8,24},{10,26},{12,28},{14,30},{1,17},... | collective-permute-start | bytes 884744 | tf_op jit(solution)/shard_map/ppermute | solution.py:397
  66.4 10.8 %collective-permute-done.10.refs_3_ = bf16[144,1024]{1,0:T(8,128)(2,1)S(1)} collective-permute-done((bf16[144,1024]{1,0:T(8,128)(2,1)}, bf16[144,1024]{1,0:T(8,128)(2,1)S(1)}, u32[]{:S(2)}, u32[]{:S(2)}) %collective-permute-start.10) | collective-permute-done | bytes 294944 | tf_op jit(solution)/shard_map/ppermute | solution.py:397
  77.2 6.5 %collective-permute-start.12 = (bf16[256,4096]{1,0:T(8,128)(2,1)}, bf16[256,4096]{1,0:T(8,128)(2,1)}, u32[]{:S(2)}, u32[]{:S(2)}) collective-permute-start(bf16[256,4096]{1,0:T(8,128)(2,1)} %collective-permute-done.11.refs_29_), channel_id=1, source_target_pairs={{0,24},{2,26},{4,28},{6,30},{8,0},{10,2},{12,4},{14,6},{16,8},{18,... | collective-permute-start | bytes 6291464 | tf_op jit(solution)/shard_map/ppermute | solution.py:405
  83.7 7.9 %collective-permute-done.3.refs_1_.refs_2_.refs_3_.refs_4_.refs_5_.refs_6_.refs_7_.refs_8_.refs_17_.refs_21_ = bf16[256,4480]{1,0:T(8,128)(2,1)S(1)} collective-permute-done((bf16[256,4480]{1,0:T(8,128)(2,1)S(1)}, bf16[256,4480]{1,0:T(8,128)(2,1)S(1)}, u32[]{:S(2)}, u32[]{:S(2)}) %collective-permute-start.3) | collective-permute-done | bytes 2293792 | tf_op jit(solution)/shard_map/ppermute | solution.py:394
  95.4 8.0 %tokens.6 = (bf16[256,4096]{1,0:T(8,128)(2,1)}, bf16[4,128,1024]{2,1,0:T(8,128)(2,1)}, f32[1,4096]{1,0:T(1,128)}, f32[256,128]{1,0:T(8,128)}) custom-call(s32[3]{0:T(128)} %pad_add_fusion.refs_0_.at.q, bf16[256,4480]{1,0:T(8,128)(2,1)} %copy-done.3, bf16[256,4480]{1,0:T(8,128)(2,1)} %copy-done.3, bf16[256,4480]{1,0:T(8,128)(2,1)} %copy-done.3, ...), custom_call_target="tpu_custom_call" | custom-call | tf_op jit(solution)/shard_map/tokens/pallas_call | solution.py:468
  103.4 8.0 %tokens.5 = (bf16[256,4096]{1,0:T(8,128)(2,1)}, bf16[4,128,1024]{2,1,0:T(8,128)(2,1)}, f32[1,4096]{1,0:T(1,128)}, f32[256,128]{1,0:T(8,128)}) custom-call(s32[3]{0:T(128)} %pad_add_fusion.refs_0_.at.q, bf16[256,4480]{1,0:T(8,128)(2,1)} %copy-done.2, bf16[256,4480]{1,0:T(8,128)(2,1)} %copy-done.2, bf16[256,4480]{1,0:T(8,128)(2,1)} %copy-done.2, ...), custom_call_target="tpu_custom_call" | custom-call | tf_op jit(solution)/shard_map/tokens/pallas_call | solution.py:468
  111.3 5.4 %collective-permute-done.5.refs_1_.refs_3_.refs_5_.refs_7_.refs_19_ = bf16[128,4480]{1,0:T(8,128)(2,1)S(1)} collective-permute-done((bf16[128,4480]{1,0:T(8,128)(2,1)S(1)}, bf16[128,4480]{1,0:T(8,128)(2,1)S(1)}, u32[]{:S(2)}, u32[]{:S(2)}) %collective-permute-start.5) | collective-permute-done | bytes 1146912 | tf_op jit(solution)/shard_map/ppermute | solution.py:394
  116.7 1.8 collective-permute-done.6.refs_2_.refs_4_.refs_6_.refs_8_.refs_23_.refs_7_
  119.5 8.0 %tokens.7 = (bf16[256,4096]{1,0:T(8,128)(2,1)}, bf16[4,128,1024]{2,1,0:T(8,128)(2,1)}, f32[1,4096]{1,0:T(1,128)}, f32[256,128]{1,0:T(8,128)}) custom-call(s32[3]{0:T(128)} %pad_add_fusion.refs_0_.at.q, bf16[128,4480]{1,0:T(8,128)(2,1)} %copy-done.4, bf16[128,4480]{1,0:T(8,128)(2,1)} %copy-done.5, bf16[128,4480]{1,0:T(8,128)(2,1)} %copy-done.4, ...), custom_call_target="tpu_custom_call" | custom-call | tf_op jit(solution)/shard_map/tokens/pallas_call | solution.py:468
  128.5 4.0 %collective-permute-start.20 = (bf16[256,4096]{1,0:T(8,128)(2,1)}, bf16[256,4096]{1,0:T(8,128)(2,1)S(1)}, u32[]{:S(2)}, u32[]{:S(2)}) collective-permute-start(bf16[256,4096]{1,0:T(8,128)(2,1)} %collective-permute-done.12.refs_30_), channel_id=1, source_target_pairs={{0,24},{2,26},{4,28},{6,30},{8,0},{10,2},{12,4},{14,6},{16,8},{18,... | collective-permute-start | bytes 6291464 | tf_op jit(solution)/shard_map/ppermute | solution.py:405
  132.5 2.8 %merge.3 = (bf16[144,1024]{1,0:T(8,128)(2,1)}, bf16[144,1024]{1,0:T(8,128)(2,1)}) custom-call(s32[3]{0:T(128)} %pad_add_fusion.refs_0_.at.q, bf16[144,1024]{1,0:T(8,128)(2,1)} %copy-done.9, bf16[144,1024]{1,0:T(8,128)(2,1)} %copy-done.16, bf16[144,1024]{1,0:T(8,128)(2,1)} %copy-done.10, bf16[144,1024]{1,0:T(8,128)(2,1)} %copy-done.15), custom_call_target="tpu_custom_call" | custom-call | tf_op jit(solution)/shard_map/merge/pallas_call | solution.py:494
  136.5 1.7 collective-permute-start.14
  138.3 6.2 %ring_grads.1 = (bf16[4,128,1024]{2,1,0:T(8,128)(2,1)}, bf16[4,128,1024]{2,1,0:T(8,128)(2,1)}, bf16[4,128,1024]{2,1,0:T(8,128)(2,1)}, bf16[4,128,1024]{2,1,0:T(8,128)(2,1)}) custom-call(s32[3]{0:T(128)} %pad_add_fusion.refs_0_.at.q, bf16[4,128,1024]{2,1,0:T(8,128)(2,1)} %get-tuple-element.81.refs_0_, bf16[4,128,1024]{2,1,0:T(8,128)(2,1)} %get-tuple-element.82.refs_1_, ...), custom_call_target="tpu_custom_call" | custom-call | tf_op jit(solution)/shard_map/ring_grads/pallas_call | solution.py:534
  144.5 5.6 %collective-permute-done.15.refs_11_ = bf16[144,1024]{1,0:T(8,128)(2,1)S(1)} collective-permute-done((bf16[144,1024]{1,0:T(8,128)(2,1)}, bf16[144,1024]{1,0:T(8,128)(2,1)S(1)}, u32[]{:S(2)}, u32[]{:S(2)}) %collective-permute-start.15) | collective-permute-done | bytes 294944 | tf_op jit(solution)/shard_map/ppermute | solution.py:394
  150.8 21.1 %finish.1 = (bf16[1024,4096]{1,0:T(8,128)(2,1)}, bf16[256,4096]{1,0:T(8,128)(2,1)}, f32[256,128]{1,0:T(8,128)}, bf16[4,2,256,256]{3,2,1,0:T(8,128)(2,1)}, bf16[4,2,256,256]{3,2,1,0:T(8,128)(2,1)}) custom-call(s32[3]{0:T(128)} %pad_add_fusion.refs_0_.at.q, bf16[256,4096]{1,0:T(8,128)(2,1)} %get-tuple-element.63.refs_0_, ...), custom_call_target="tpu_custom_call" | custom-call | tf_op jit(solution)/shard_map/finish/pallas_call | solution.py:549
  171.9 2.9 %collective-permute-start.16 = (bf16[4,2,256,256]{3,2,1,0:T(8,128)(2,1)}, bf16[4,2,256,256]{3,2,1,0:T(8,128)(2,1)S(1)}, u32[]{:S(2)}, u32[]{:S(2)}) collective-permute-start(bf16[4,2,256,256]{3,2,1,0:T(8,128)(2,1)} %get-tuple-element.110), channel_id=1, source_target_pairs={{0,1},{1,0},{2,3},{3,2},{4,5},{5,4},{6,7},{7,6},{8,9},{9,8},{10,11... | collective-permute-start | bytes 3145736 | tf_op jit(solution)/shard_map/ppermute | solution.py:614
  174.8 6.4 %read_carry.1 = (bf16[256,128]{1,0:T(8,128)(2,1)}, bf16[256,128]{1,0:T(8,128)(2,1)}, bf16[256,128]{1,0:T(8,128)(2,1)}, bf16[256,128]{1,0:T(8,128)(2,1)}) custom-call(s32[3]{0:T(128)} %pad_add_fusion.refs_0_.at.q, bf16[256,4480]{1,0:T(8,128)(2,1)} %pack.1.refs_1_.refs_2_.refs_3_.refs_4_.refs_5_.refs_6_.refs_7_.refs_8_.refs_16_.refs_20_.refs_0_, ...), custom_call_target="tpu_custom_call" | custom-call | tf_op jit(solution)/shard_map/read_carry/pallas_call | solution.py:583
  190.0 5.7 %convolution_convert_fusion = bf16[1024,256]{1,0:T(8,128)(2,1)S(1)} fusion(bf16[1024,4096]{1,0:T(8,128)(2,1)} %get-tuple-element.111, bf16[256,4096]{1,0:T(8,128)(2,1)S(1)} %collective-permute-done.20), kind=kOutput, calls=%fused_computation.1 | convolution fusion | flops 2147745792 | bytes 11010048 | tf_op jit(solution)/shard_map/dot_general | solution.py:20
  200.2 3.3 %collective-permute-start.22 = (bf16[256,256]{1,0:T(8,128)(2,1)S(1)}, bf16[256,256]{1,0:T(8,128)(2,1)S(1)}, u32[]{:S(2)}, u32[]{:S(2)}) collective-permute-start(bf16[256,256]{1,0:T(8,128)(2,1)S(1)} %get-tuple-element.128), channel_id=1, source_target_pairs={{1,3},{3,1},{5,7},{7,5},{8,10},{10,8},{12,14},{14,12},{16,18},{18,... | collective-permute-start | bytes 393224 | tf_op jit(solution)/shard_map/ppermute | solution.py:628
  203.5 2.1 collective-permute-start.23
  205.7 2.9 %collective-permute-start.24 = (bf16[256,256]{1,0:T(8,128)(2,1)S(1)}, bf16[256,256]{1,0:T(8,128)(2,1)S(1)}, u32[]{:S(2)}, u32[]{:S(2)}) collective-permute-start(bf16[256,256]{1,0:T(8,128)(2,1)S(1)} %get-tuple-element.126), channel_id=1, source_target_pairs={{1,7},{3,5},{5,3},{7,1},{8,14},{10,12},{12,10},{14,8},{16,22},{18,... | collective-permute-start | bytes 393224 | tf_op jit(solution)/shard_map/ppermute | solution.py:628
  210.4 2.0 collective-permute-done.22.refs_5_
  212.4 2.8 %collective-permute-done.23.refs_6_ = bf16[256,256]{1,0:T(8,128)(2,1)S(1)} collective-permute-done((bf16[256,256]{1,0:T(8,128)(2,1)S(1)}, bf16[256,256]{1,0:T(8,128)(2,1)S(1)}, u32[]{:S(2)}, u32[]{:S(2)}) %collective-permute-start.23) | collective-permute-done | bytes 131104 | tf_op jit(solution)/shard_map/ppermute | solution.py:628
  (94 shorter events, 36.9 us)
Async XLA Ops:
  0.6 76.6 %collective-permute-start.11 = (bf16[256,4096]{1,0:T(8,128)(2,1)}, bf16[256,4096]{1,0:T(8,128)(2,1)}, u32[]{:S(2)}, u32[]{:S(2)}) collective-permute-start(bf16[256,4096]{1,0:T(8,128)(2,1)} %refs_28_.1), channel_id=1, source_target_pairs={{0,24},{2,26},{4,28},{6,30},{8,0},{10,2},{12,4},{14,6},{16,8},{18,... | collective-permute-start | bytes 6291464 | tf_op jit(solution)/shard_map/ppermute | solution.py:405
  15.1 22.9 %collective-permute-start = (bf16[272,1024]{1,0:T(8,128)(2,1)}, bf16[272,1024]{1,0:T(8,128)(2,1)S(1)}, u32[]{:S(2)}, u32[]{:S(2)}) collective-permute-start(bf16[272,1024]{1,0:T(8,128)(2,1)} %get-tuple-element.65), channel_id=1, source_target_pairs={{0,2},{2,0},{4,6},{6,4},{8,10},{10,8},{12,14},{14,12},{16,18},{18,... | collective-permute-start | bytes 1671176 | tf_op jit(solution)/shard_map/ppermute | solution.py:394
  16.3 21.7 %collective-permute-start.1 = (bf16[272,1024]{1,0:T(8,128)(2,1)}, bf16[272,1024]{1,0:T(8,128)(2,1)S(1)}, u32[]{:S(2)}, u32[]{:S(2)}) collective-permute-start(bf16[272,1024]{1,0:T(8,128)(2,1)} %get-tuple-element.66), channel_id=1, source_target_pairs={{0,4},{2,6},{4,0},{6,2},{8,12},{10,14},{12,8},{14,10},{16,20},{18,... | collective-permute-start | bytes 1671176 | tf_op jit(solution)/shard_map/ppermute | solution.py:394
  17.5 23.9 %collective-permute-start.2 = (bf16[272,1024]{1,0:T(8,128)(2,1)}, bf16[272,1024]{1,0:T(8,128)(2,1)S(1)}, u32[]{:S(2)}, u32[]{:S(2)}) collective-permute-start(bf16[272,1024]{1,0:T(8,128)(2,1)} %get-tuple-element.67), channel_id=1, source_target_pairs={{0,6},{2,4},{4,2},{6,0},{8,14},{10,12},{12,10},{14,8},{16,22},{18,... | collective-permute-start | bytes 1671176 | tf_op jit(solution)/shard_map/ppermute | solution.py:394
  42.2 49.3 %collective-permute-start.3 = (bf16[256,4480]{1,0:T(8,128)(2,1)S(1)}, bf16[256,4480]{1,0:T(8,128)(2,1)S(1)}, u32[]{:S(2)}, u32[]{:S(2)}) collective-permute-start(bf16[256,4480]{1,0:T(8,128)(2,1)S(1)} %copy-done.1), channel_id=1, source_target_pairs={{0,2},{2,0},{4,6},{6,4},{8,10},{10,8},{12,14},{14,12},{16,18},{18,... | collective-permute-start | bytes 6881288 | tf_op jit(solution)/shard_map/ppermute | solution.py:394
  43.4 49.3 %collective-permute-start.4 = (bf16[256,4480]{1,0:T(8,128)(2,1)S(1)}, bf16[256,4480]{1,0:T(8,128)(2,1)S(1)}, u32[]{:S(2)}, u32[]{:S(2)}) collective-permute-start(bf16[256,4480]{1,0:T(8,128)(2,1)S(1)} %copy-done.1), channel_id=1, source_target_pairs={{0,4},{2,6},{4,0},{6,2},{8,12},{10,14},{12,8},{14,10},{16,20},{18,... | collective-permute-start | bytes 6881288 | tf_op jit(solution)/shard_map/ppermute | solution.py:394
  47.1 8.3 %collective-permute-start.7 = (bf16[144,1024]{1,0:T(8,128)(2,1)}, bf16[144,1024]{1,0:T(8,128)(2,1)S(1)}, u32[]{:S(2)}, u32[]{:S(2)}) collective-permute-start(bf16[144,1024]{1,0:T(8,128)(2,1)} %get-tuple-element.89.refs_0_), channel_id=1, source_target_pairs={{0,8},{2,10},{4,12},{6,14},{8,16},{10,18},{12,20},{14,22},{16,24},... | collective-permute-start | bytes 884744 | tf_op jit(solution)/shard_map/ppermute | solution.py:397
  48.4 8.0 %collective-permute-start.8 = (bf16[144,1024]{1,0:T(8,128)(2,1)}, bf16[144,1024]{1,0:T(8,128)(2,1)S(1)}, u32[]{:S(2)}, u32[]{:S(2)}) collective-permute-start(bf16[144,1024]{1,0:T(8,128)(2,1)} %get-tuple-element.90.refs_2_), channel_id=1, source_target_pairs={{8,0},{10,2},{12,4},{14,6},{16,8},{18,10},{20,12},{22,14},{24,16},... | collective-permute-start | bytes 884744 | tf_op jit(solution)/shard_map/ppermute | solution.py:397
  59.9 17.3 %collective-permute-start.10 = (bf16[144,1024]{1,0:T(8,128)(2,1)}, bf16[144,1024]{1,0:T(8,128)(2,1)S(1)}, u32[]{:S(2)}, u32[]{:S(2)}) collective-permute-start(bf16[144,1024]{1,0:T(8,128)(2,1)} %get-tuple-element.92), channel_id=1, source_target_pairs={{16,0},{18,2},{20,4},{22,6},{24,8},{26,10},{28,12},{30,14},{17,1},... | collective-permute-start | bytes 884744 | tf_op jit(solution)/shard_map/ppermute | solution.py:397
  61.2 16.0 %collective-permute-start.9 = (bf16[144,1024]{1,0:T(8,128)(2,1)}, bf16[144,1024]{1,0:T(8,128)(2,1)S(1)}, u32[]{:S(2)}, u32[]{:S(2)}) collective-permute-start(bf16[144,1024]{1,0:T(8,128)(2,1)} %get-tuple-element.91), channel_id=1, source_target_pairs={{0,16},{2,18},{4,20},{6,22},{8,24},{10,26},{12,28},{14,30},{1,17},... | collective-permute-start | bytes 884744 | tf_op jit(solution)/shard_map/ppermute | solution.py:397
  77.2 26.1 %copy-start.15 = (bf16[144,1024]{1,0:T(8,128)(2,1)}, bf16[144,1024]{1,0:T(8,128)(2,1)S(1)}, u32[]{:S(2)}) copy-start(bf16[144,1024]{1,0:T(8,128)(2,1)S(1)} %collective-permute-done.10.refs_3_) | copy-start | bytes 884740
  77.2 14.3 %copy-start.16 = (bf16[144,1024]{1,0:T(8,128)(2,1)}, bf16[144,1024]{1,0:T(8,128)(2,1)S(1)}, u32[]{:S(2)}) copy-start(bf16[144,1024]{1,0:T(8,128)(2,1)S(1)} %collective-permute-done.9.refs_1_) | copy-start | bytes 884740
  77.2 51.3 %collective-permute-start.12 = (bf16[256,4096]{1,0:T(8,128)(2,1)}, bf16[256,4096]{1,0:T(8,128)(2,1)}, u32[]{:S(2)}, u32[]{:S(2)}) collective-permute-start(bf16[256,4096]{1,0:T(8,128)(2,1)} %collective-permute-done.11.refs_29_), channel_id=1, source_target_pairs={{0,24},{2,26},{4,28},{6,30},{8,0},{10,2},{12,4},{14,6},{16,8},{18,... | collective-permute-start | bytes 6291464 | tf_op jit(solution)/shard_map/ppermute | solution.py:405
  92.8 24.0 %collective-permute-start.5 = (bf16[128,4480]{1,0:T(8,128)(2,1)S(1)}, bf16[128,4480]{1,0:T(8,128)(2,1)S(1)}, u32[]{:S(2)}, u32[]{:S(2)}) collective-permute-start(bf16[128,4480]{1,0:T(8,128)(2,1)S(1)} %slice.40), channel_id=1, source_target_pairs={{0,4},{2,6},{4,0},{6,2},{8,12},{10,14},{12,8},{14,10},{16,20},{18,... | collective-permute-start | bytes 3440648 | tf_op jit(solution)/shard_map/ppermute | solution.py:394
  94.4 24.1 %collective-permute-start.6 = (bf16[128,4480]{1,0:T(8,128)(2,1)}, bf16[128,4480]{1,0:T(8,128)(2,1)S(1)}, u32[]{:S(2)}, u32[]{:S(2)}) collective-permute-start(bf16[128,4480]{1,0:T(8,128)(2,1)} %slice.41), channel_id=1, source_target_pairs={{0,2},{2,0},{4,6},{6,4},{8,10},{10,8},{12,14},{14,12},{16,18},{18,... | collective-permute-start | bytes 3440648 | tf_op jit(solution)/shard_map/ppermute | solution.py:394
  128.5 61.5 %collective-permute-start.20 = (bf16[256,4096]{1,0:T(8,128)(2,1)}, bf16[256,4096]{1,0:T(8,128)(2,1)S(1)}, u32[]{:S(2)}, u32[]{:S(2)}) collective-permute-start(bf16[256,4096]{1,0:T(8,128)(2,1)} %collective-permute-done.12.refs_30_), channel_id=1, source_target_pairs={{0,24},{2,26},{4,28},{6,30},{8,0},{10,2},{12,4},{14,6},{16,8},{18,... | collective-permute-start | bytes 6291464 | tf_op jit(solution)/shard_map/ppermute | solution.py:405
  135.3 9.1 %collective-permute-start.13 = (bf16[144,1024]{1,0:T(8,128)(2,1)}, bf16[144,1024]{1,0:T(8,128)(2,1)S(1)}, u32[]{:S(2)}, u32[]{:S(2)}) collective-permute-start(bf16[144,1024]{1,0:T(8,128)(2,1)} %get-tuple-element.103.refs_8_), channel_id=1, source_target_pairs={{0,2},{2,0},{4,6},{6,4},{8,10},{10,8},{12,14},{14,12},{16,18},{18,... | collective-permute-start | bytes 884744 | tf_op jit(solution)/shard_map/ppermute | solution.py:394
  136.5 7.9 %collective-permute-start.14 = (bf16[144,1024]{1,0:T(8,128)(2,1)}, bf16[144,1024]{1,0:T(8,128)(2,1)S(1)}, u32[]{:S(2)}, u32[]{:S(2)}) collective-permute-start(bf16[144,1024]{1,0:T(8,128)(2,1)} %get-tuple-element.103.refs_8_), channel_id=1, source_target_pairs={{0,4},{2,6},{4,0},{6,2},{8,12},{10,14},{12,8},{14,10},{16,20},{18,... | collective-permute-start | bytes 884744 | tf_op jit(solution)/shard_map/ppermute | solution.py:394
  138.3 11.8 %collective-permute-start.15 = (bf16[144,1024]{1,0:T(8,128)(2,1)}, bf16[144,1024]{1,0:T(8,128)(2,1)S(1)}, u32[]{:S(2)}, u32[]{:S(2)}) collective-permute-start(bf16[144,1024]{1,0:T(8,128)(2,1)} %get-tuple-element.103.refs_8_), channel_id=1, source_target_pairs={{0,6},{2,4},{4,2},{6,0},{8,14},{10,12},{12,10},{14,8},{16,22},{18,... | collective-permute-start | bytes 884744 | tf_op jit(solution)/shard_map/ppermute | solution.py:394
  171.9 17.8 %collective-permute-start.16 = (bf16[4,2,256,256]{3,2,1,0:T(8,128)(2,1)}, bf16[4,2,256,256]{3,2,1,0:T(8,128)(2,1)S(1)}, u32[]{:S(2)}, u32[]{:S(2)}) collective-permute-start(bf16[4,2,256,256]{3,2,1,0:T(8,128)(2,1)} %get-tuple-element.110), channel_id=1, source_target_pairs={{0,1},{1,0},{2,3},{3,2},{4,5},{5,4},{6,7},{7,6},{8,9},{9,8},{10,11... | collective-permute-start | bytes 3145736 | tf_op jit(solution)/shard_map/ppermute | solution.py:614
  181.2 3.9 %collective-permute-start.25 = (bf16[256,128]{1,0:T(8,128)(2,1)}, bf16[256,128]{1,0:T(8,128)(2,1)S(1)}, u32[]{:S(2)}, u32[]{:S(2)}) collective-permute-start(bf16[256,128]{1,0:T(8,128)(2,1)} %get-tuple-element.119), channel_id=1, source_target_pairs={{0,2},{2,0},{4,6},{6,4},{8,10},{10,8},{12,14},{14,12},{16,18},{18,... | collective-permute-start | bytes 196616 | tf_op jit(solution)/shard_map/ppermute | solution.py:394
  182.4 3.3 %collective-permute-start.26 = (bf16[256,128]{1,0:T(8,128)(2,1)}, bf16[256,128]{1,0:T(8,128)(2,1)S(1)}, u32[]{:S(2)}, u32[]{:S(2)}) collective-permute-start(bf16[256,128]{1,0:T(8,128)(2,1)} %get-tuple-element.120), channel_id=1, source_target_pairs={{0,4},{2,6},{4,0},{6,2},{8,12},{10,14},{12,8},{14,10},{16,20},{18,... | collective-permute-start | bytes 196616 | tf_op jit(solution)/shard_map/ppermute | solution.py:394
  182.8 4.4 %collective-permute-start.27 = (bf16[256,128]{1,0:T(8,128)(2,1)}, bf16[256,128]{1,0:T(8,128)(2,1)S(1)}, u32[]{:S(2)}, u32[]{:S(2)}) collective-permute-start(bf16[256,128]{1,0:T(8,128)(2,1)} %get-tuple-element.121), channel_id=1, source_target_pairs={{0,6},{2,4},{4,2},{6,0},{8,14},{10,12},{12,10},{14,8},{16,22},{18,... | collective-permute-start | bytes 196616 | tf_op jit(solution)/shard_map/ppermute | solution.py:394
  188.1 8.9 %collective-permute-start.28 = (f32[2,256,128]{2,1,0:T(8,128)S(1)}, f32[2,256,128]{2,1,0:T(8,128)S(1)}, u32[]{:S(2)}, u32[]{:S(2)}) collective-permute-start(f32[2,256,128]{2,1,0:T(8,128)S(1)} %pad_maximum_fusion), channel_id=1, source_target_pairs={{0,1},{1,0},{2,3},{3,2},{4,5},{5,4},{6,7},{7,6},{8,9},{9,8},{10,11... | collective-permute-start | bytes 786440 | tf_op jit(solution)/shard_map/ppermute | solution.py:605
  195.8 4.2 %collective-permute-start.21 = (bf16[1024,256]{1,0:T(8,128)(2,1)S(1)}, bf16[1024,256]{1,0:T(8,128)(2,1)S(1)}, u32[]{:S(2)}, u32[]{:S(2)}) collective-permute-start(bf16[1024,256]{1,0:T(8,128)(2,1)S(1)} %convolution_convert_fusion), channel_id=1, source_target_pairs={{0,1},{2,3},{4,5},{6,7},{9,8},{11,10},{13,12},{15,14},{17,16},{19,... | collective-permute-start | bytes 1572872 | tf_op jit(solution)/shard_map/ppermute | solution.py:623
  197.2 18.0 %copy-start = (s32[3]{0:T(128)S(1)}, s32[3]{0:T(128)}, u32[]{:S(2)}) copy-start(s32[3]{0:T(128)} %pad_add_fusion.refs_0_.at.q) | copy-start | bytes 40
  197.2 8.4 %collective-permute-start.17 = (bf16[2,256,256]{2,1,0:T(8,128)(2,1)S(1)}, bf16[2,256,256]{2,1,0:T(8,128)(2,1)S(1)}, u32[]{:S(2)}, u32[]{:S(2)}) collective-permute-start(bf16[2,256,256]{2,1,0:T(8,128)(2,1)S(1)} %get-tuple-element.124), channel_id=1, source_target_pairs={{0,2},{2,0},{4,6},{6,4},{8,10},{10,8},{12,14},{14,12},{16,18},{18,... | collective-permute-start | bytes 786440 | tf_op jit(solution)/shard_map/ppermute | solution.py:394
  198.8 10.6 %collective-permute-start.18 = (bf16[2,256,256]{2,1,0:T(8,128)(2,1)S(1)}, bf16[2,256,256]{2,1,0:T(8,128)(2,1)S(1)}, u32[]{:S(2)}, u32[]{:S(2)}) collective-permute-start(bf16[2,256,256]{2,1,0:T(8,128)(2,1)S(1)} %get-tuple-element.123), channel_id=1, source_target_pairs={{0,4},{2,6},{4,0},{6,2},{8,12},{10,14},{12,8},{14,10},{16,20},{18,... | collective-permute-start | bytes 786440 | tf_op jit(solution)/shard_map/ppermute | solution.py:394
  199.0 11.4 %collective-permute-start.19 = (bf16[2,256,256]{2,1,0:T(8,128)(2,1)S(1)}, bf16[2,256,256]{2,1,0:T(8,128)(2,1)S(1)}, u32[]{:S(2)}, u32[]{:S(2)}) collective-permute-start(bf16[2,256,256]{2,1,0:T(8,128)(2,1)S(1)} %get-tuple-element.122), channel_id=1, source_target_pairs={{0,6},{2,4},{4,2},{6,0},{8,14},{10,12},{12,10},{14,8},{16,22},{18,... | collective-permute-start | bytes 786440 | tf_op jit(solution)/shard_map/ppermute | solution.py:394
  200.2 12.2 %collective-permute-start.22 = (bf16[256,256]{1,0:T(8,128)(2,1)S(1)}, bf16[256,256]{1,0:T(8,128)(2,1)S(1)}, u32[]{:S(2)}, u32[]{:S(2)}) collective-permute-start(bf16[256,256]{1,0:T(8,128)(2,1)S(1)} %get-tuple-element.128), channel_id=1, source_target_pairs={{1,3},{3,1},{5,7},{7,5},{8,10},{10,8},{12,14},{14,12},{16,18},{18,... | collective-permute-start | bytes 393224 | tf_op jit(solution)/shard_map/ppermute | solution.py:628
  203.5 11.7 %collective-permute-start.23 = (bf16[256,256]{1,0:T(8,128)(2,1)S(1)}, bf16[256,256]{1,0:T(8,128)(2,1)S(1)}, u32[]{:S(2)}, u32[]{:S(2)}) collective-permute-start(bf16[256,256]{1,0:T(8,128)(2,1)S(1)} %get-tuple-element.127), channel_id=1, source_target_pairs={{1,5},{3,7},{5,1},{7,3},{8,12},{10,14},{12,8},{14,10},{16,20},{18,... | collective-permute-start | bytes 393224 | tf_op jit(solution)/shard_map/ppermute | solution.py:628
  205.7 9.6 %collective-permute-start.24 = (bf16[256,256]{1,0:T(8,128)(2,1)S(1)}, bf16[256,256]{1,0:T(8,128)(2,1)S(1)}, u32[]{:S(2)}, u32[]{:S(2)}) collective-permute-start(bf16[256,256]{1,0:T(8,128)(2,1)S(1)} %get-tuple-element.126), channel_id=1, source_target_pairs={{1,7},{3,5},{5,3},{7,1},{8,14},{10,12},{12,10},{14,8},{16,22},{18,... | collective-permute-start | bytes 393224 | tf_op jit(solution)/shard_map/ppermute | solution.py:628
  (17 other events, 92.7 us)
